TPU v7x, 256 devices: a whole 4x4x8 slice. The times are simulated.
256 devices in a mesh: view: 4 (over z_hi), block: 64 (over y, x, z_lo, core).
Axes of the slice: x: 4, y: 4, z: 8 (z_hi: 4, z_lo: 2; z = z_hi * 2 + z_lo), core: 2. Of those that a mesh axis runs over, the one named last changes fastest.
Arguments:
- view_tiles: bfloat16 [4, 5120, 24, 1024], P('view', 'block'), may hold values from 0.25 to 4
- route_block: int32 [4, 5120], P('view', 'block'), may hold values from 0 to 63, as said below
- route_column: int32 [4, 5120], P('view', 'block'), may hold values from 0 to 31, as said below
- psf_taps: float32 [4, 3, 31], P('view'), may hold values from 0.002 to 1.5
- start_estimate: float32 [24, 2048, 1024], P(None, 'block'), may hold values from 0.5 to 2
Outputs:
- estimate: float32 [24, 2048, 1024], P(None, 'block')
Inputs may be any that keep to these rules, and one draw needn't show every extreme that they name: `route_block`: for each view, every column of every block receives at least one tile column; at most 2 tile columns held by one device go to one block, and in every draw some block receives exactly 2 from every device. `route_column`: column within the receiving block.
All inputs are finite; a program needn't handle non-finite values.
Results may differ from a plain program's by a relative error of at most 0.00071.
Values may be sent and summed in bfloat16 or wider, within the bound.
No kernel may reach another device: no remote copies, remote signals or barrier semaphores. Data moves between devices by JAX's collectives and lax.ppermute only.
A program may use at most 128 MiB of HBM per device.

v0:
```python
import jax
import jax.numpy as jnp
from jax import lax
from jax.sharding import PartitionSpec as P

ITERS = 2
HALF = 15


def padded(cells, sides, width):
    for axis, dim in sides:
        count = lax.axis_size(axis)
        ends = count - 1
        head = lax.slice_in_dim(cells, 0, width, axis=dim)
        tail = lax.slice_in_dim(cells, cells.shape[dim] - width, cells.shape[dim], axis=dim)
        cells = jnp.concatenate(
            [
                lax.ppermute(tail, axis, [(i, (i + 1) % count) for i in range(ends)]),
                cells,
                lax.ppermute(head, axis, [((i + 1) % count, i) for i in range(ends)]),
            ],
            axis=dim,
        )
    return cells


def banded(tap_weights, size_in, size_out, offset):
    margin = (tap_weights.shape[0] - 1) // 2
    rows_in = lax.broadcasted_iota(jnp.int32, (size_in, size_out), 0)
    cols_out = lax.broadcasted_iota(jnp.int32, (size_in, size_out), 1)
    distance = rows_in - cols_out - offset + margin
    matrix = jnp.zeros((size_in, size_out), jnp.float32)
    for tap_index in range(tap_weights.shape[0]):
        matrix = matrix + jnp.where(distance == tap_index, tap_weights[tap_index], 0.0)
    return matrix.astype(jnp.bfloat16)


def across_columns(field, matrix):
    return jnp.einsum(
        "zxy,xw->zwy", field.astype(jnp.bfloat16), matrix, preferred_element_type=jnp.float32
    )


def across_rows(field, matrix):
    return jnp.einsum(
        "zxy,yw->zxw", field.astype(jnp.bfloat16), matrix, preferred_element_type=jnp.float32
    )


def across_depth(field, matrix):
    return jnp.einsum(
        "zxy,zw->wxy", field.astype(jnp.bfloat16), matrix, preferred_element_type=jnp.float32
    )


def mirror_rows(field, matrix):
    return jnp.einsum(
        "zxy,wy->zxw", field.astype(jnp.bfloat16), matrix, preferred_element_type=jnp.float32
    )


def mirror_depth(field, matrix):
    return jnp.einsum(
        "zxy,wz->wxy", field.astype(jnp.bfloat16), matrix, preferred_element_type=jnp.float32
    )


def per_device(view_tiles, route_block, route_column, psf_taps, start_estimate):
    groups = lax.axis_size("block")
    width_block = start_estimate.shape[1]
    capacity = max(2, (2 * width_block + groups - 1) // groups)
    pieces = view_tiles[0]
    blocks = route_block[0]
    columns = route_column[0]
    depth = pieces.shape[1]
    rows_y = pieces.shape[2]
    onehot = (blocks[:, None] == jnp.arange(groups, dtype=jnp.int32)[None, :]).astype(jnp.int32)
    earlier = jnp.cumsum(onehot, axis=0) - onehot
    rank_in = jnp.sum(earlier * onehot, axis=1)
    slot_of = blocks * capacity + rank_in
    outgoing = jnp.zeros((groups * capacity, depth, rows_y), jnp.bfloat16).at[slot_of].set(pieces)
    labels = jnp.zeros((groups * capacity,), jnp.int32).at[slot_of].set(columns + 1)
    arrived, arrived_labels = (
        lax.all_to_all(
            outgoing.reshape(groups, capacity, depth, rows_y),
            "block",
            split_axis=0,
            concat_axis=0,
            tiled=True,
        ),
        lax.all_to_all(
            labels.reshape(groups, capacity), "block", split_axis=0, concat_axis=0, tiled=True
        ),
    )
    arrived = arrived.reshape(groups * capacity, depth, rows_y)
    wanted = jnp.arange(width_block, dtype=jnp.int32) + 1
    selector = arrived_labels.reshape(groups * capacity)[:, None] == wanted[None, :]
    summed = jnp.einsum(
        "sk,szy->zky", selector.astype(jnp.bfloat16), arrived, preferred_element_type=jnp.float32
    )
    covered = jnp.sum(selector.astype(jnp.float32), axis=0)
    measured = summed / covered[None, :, None]
    kernel = psf_taps[0] / jnp.sum(psf_taps[0], axis=1, keepdims=True)
    reversed_kernel = kernel[:, ::-1]
    rows_band = banded(kernel[2], rows_y, rows_y, 0)
    depth_band = banded(kernel[0], depth, depth, 0)
    back_cols = banded(reversed_kernel[1], width_block + 2 * HALF, width_block, HALF)
    fore_cols = banded(kernel[1], width_block + 2 * HALF, width_block, HALF)
    views_count = lax.axis_size("view")
    estimate = start_estimate
    for iteration in range(ITERS):
        widened = padded(estimate.astype(jnp.bfloat16), (("block", 1),), HALF).astype(
            estimate.dtype
        )
        blurred = across_depth(
            across_rows(across_columns(widened, fore_cols), rows_band), depth_band
        )
        quotient = measured / blurred
        quotient_wide = padded(quotient.astype(jnp.bfloat16), (("block", 1),), HALF).astype(
            quotient.dtype
        )
        partial_value = mirror_depth(
            mirror_rows(across_columns(quotient_wide, back_cols), rows_band), depth_band
        )
        summed_views = lax.psum(partial_value, "view")
        estimate = estimate * summed_views / views_count
    return estimate


def solution(mesh):
    placed = (
        P("view", "block", None, None),
        P("view", "block"),
        P("view", "block"),
        P("view", None, None),
        P(None, "block", None),
    )
    return jax.shard_map(
        per_device, mesh=mesh, in_specs=placed, out_specs=P(None, "block", None), check_vma=False
    )
```

profile of v0, /device:TPU:58, one launch (start us, length us, event | category | flops | bytes accessed | tf_op | source)
XLA Modules:
  0.0 735.3 jit_solution(9513635687173732299)
XLA Ops:
  6.5 0.7 add_bitcast_fusion
  7.2 0.7 fusion.132
  8.0 0.8 select_reduce_fusion
  8.9 0.7 fusion.238
  9.6 0.8 scatter_custom_fusion.1
  10.4 0.8 all_to_all.10
  11.1 8.8 %all-to-all-start.1 = ((s32[64,1,2]{2,1,0:T(1,128)}), s32[64,1,2]{2,1,0:T(1,128)S(1)}, u32[]{:S(2)}, u32[]{:S(2)}) async-start(s32[64,1,2]{2,1,0:T(1,128)} %bitcast.71), calls=%async_computation.1 | async-start | bytes 65536 | tf_op jit(solution)/shard_map/all_to_all | solution.py:91
  20.0 3.5 broadcast_in_dim.522
  23.4 13.7 %scatter_fusion = bf16[128,24,1024]{2,1,0:T(8,128)(2,1)} fusion(bf16[128,24,1024]{2,1,0:T(8,128)(2,1)} %broadcast_in_dim.522, s32[80]{0:T(128)S(1)} %fusion.238, bf16[80,24,1024]{2,1,0:T(8,128)(2,1)} %bitcast.173), kind=kCustom, calls=%fused_computation | custom fusion | bytes 11796800 | tf_op jit(solution)/shard_map/scatter | solution.py:81
  37.1 12.7 %copy.19 = bf16[64,2,24,1024]{3,1,2,0:T(2,128)(2,1)} copy(bf16[64,2,24,1024]{3,2,1,0:T(8,128)(2,1)} %bitcast.172) | data formatting | bytes 12582912 | tf_op jit(solution)/shard_map/reshape | solution.py:85
  49.9 9.2 %all-to-all-start = ((bf16[64,2,24,1024]{3,1,2,0:T(2,128)(2,1)}), bf16[64,2,24,1024]{3,1,2,0:T(2,128)(2,1)}, u32[]{:S(2)}, u32[]{:S(2)}) async-start(bf16[64,2,24,1024]{3,1,2,0:T(2,128)(2,1)} %copy.19), calls=%async_computation | async-start | bytes 12582912 | tf_op jit(solution)/shard_map/all_to_all | solution.py:84
  59.4 1.1 copy-done.1
  60.8 1.4 copy.23
  62.2 2.2 collective-permute-start.1
  64.4 1.3 copy.22
  65.7 2.6 collective-permute-start
  68.5 0.7 fusion.636
  69.2 0.7 fusion.635
  69.9 19.4 %fusion.233 = bf16[24,24,1]{1,0,2:T(8,128)(2,1)S(1)} fusion(f32[]{:T(128)} %bitcast.30, f32[]{:T(128)} %bitcast.29, f32[]{:T(128)} %bitcast.28, f32[]{:T(128)} %bitcast.27, f32[]{:T(128)} %bitcast.26, f32[]{:T(128)} %bitcast.25, f32[]{:T(128)} %bitcast.24, f32[]{:T(128)} %bitcast.23, f32[]{:T(128)} %bitcast.22, f32[]{:T(128)} %bitcast.21, f32[]{:T(128)} %bitcast.20, ...), kind=kLoop, calls=%fused_computation.213 | loop fusion | flops 54720 | bytes 1276 | tf_op jit(solution)/shard_map/convert_element_type | solution.py:35
  89.3 0.7 fusion.633
  90.1 0.7 fusion.632
  90.8 0.7 fusion.634
  91.5 0.6 broadcast.405
  92.1 0.7 reduce.4
  93.2 51.9 %collective-permute-done.1 = bf16[24,15,1024]{2,0,1:T(8,128)(2,1)} collective-permute-done((bf16[24,15,1024]{2,0,1:T(8,128)(2,1)}, bf16[24,15,1024]{2,0,1:T(8,128)(2,1)}, u32[]{:S(2)}, u32[]{:S(2)}) %collective-permute-start.1) | collective-permute-done | bytes 737312 | tf_op jit(solution)/shard_map/ppermute | solution.py:20
  145.1 1.5 copy.25
  146.6 1.5 copy.24
  148.2 22.8 %fusion.122 = bf16[24,32,1024]{2,1,0:T(8,128)(2,1)} fusion(bf16[24,15,1024]{2,1,0:T(8,128)(2,1)S(1)} %copy.25, bf16[24,32,1024]{2,1,0:T(8,128)(2,1)} %copy-done.1, bf16[24,15,1024]{2,1,0:T(8,128)(2,1)S(1)} %copy.24, f32[]{:T(128)} %bitcast.62, f32[]{:T(128)} %bitcast.61, f32[]{:T(128)} %bitcast.60, f32[]{:T(128)} %bitcast.59, f32[]{:T(128)} %bitcast.58, ...), kind=kOutput, calls=%fused_computation.99 | convolution fusion | flops 107632768 | bytes 4620412 | tf_op jit(solution)/shard_map/zxy,xw->zwy/dot_general | solution.py:39
  171.0 27.0 %fusion.79 = f32[24,32,1024]{2,0,1:T(8,128)} fusion(bf16[24,24,1]{1,0,2:T(8,128)(2,1)S(1)} %fusion.233, f32[]{:T(128)} %bitcast.107, f32[]{:T(128)} %bitcast.106, f32[]{:T(128)} %bitcast.105, f32[]{:T(128)} %bitcast.104, f32[]{:T(128)} %bitcast.103, f32[]{:T(128)} %bitcast.102, f32[]{:T(128)} %bitcast.101, f32[]{:T(128)} %bitcast.100, f32[]{:T(128)} %bitcast.99, ...), kind=kOutput, calls=%fused_computation.83 | convolution fusion | flops 1748762624 | bytes 4719868 | tf_op jit(solution)/shard_map/zxy,zw->wxy/dot_general | solution.py:51
  198.0 7.0 copy.20
  205.0 10.1 %reshape.298 = bf16[128,24,1024]{2,0,1:T(8,128)(2,1)} reshape(bf16[64,2,24,1024]{3,1,0,2:T(2,128)(2,1)} %copy.20) | data formatting | bytes 12582912 | tf_op jit(solution)/shard_map/reshape | solution.py:95
  215.2 8.8 %fusion.49 = (bf16[24,32,1024]{2,1,0:T(8,128)(2,1)S(1)}, f32[24,1024,32]{1,2,0:T(8,128)}) fusion(f32[24,32,1024]{2,0,1:T(8,128)} %fusion.79, f32[32]{0:T(128)S(1)} %fusion.133, bf16[128,24,1024]{2,0,1:T(8,128)(2,1)} %reshape.298, s32[128]{0:T(128)S(1)} %eq.676, s32[32]{0:T(128)S(1)} %iota_add_fusion), kind=kOutput, calls=%fused_computation.55 | convolution fusion | flops 203689984 | bytes 14156544 | tf_op jit(solution)/shard_map/sk,szy->zky/dot_general | solution.py:98
  224.2 0.4 copy.30
  224.7 3.8 collective-permute-start.3
  228.5 0.4 copy.29
  228.9 3.0 collective-permute-start.2
  231.9 8.0 %collective-permute-done.3 = bf16[24,15,1024]{2,0,1:T(8,128)(2,1)S(1)} collective-permute-done((bf16[24,15,1024]{2,0,1:T(8,128)(2,1)S(1)}, bf16[24,15,1024]{2,0,1:T(8,128)(2,1)S(1)}, u32[]{:S(2)}, u32[]{:S(2)}) %collective-permute-start.3) | collective-permute-done | bytes 737312 | tf_op jit(solution)/shard_map/ppermute | solution.py:20
  239.9 0.4 copy.32
  240.3 7.6 %collective-permute-done.2 = bf16[24,15,1024]{2,0,1:T(8,128)(2,1)S(1)} collective-permute-done((bf16[24,15,1024]{2,0,1:T(8,128)(2,1)S(1)}, bf16[24,15,1024]{2,0,1:T(8,128)(2,1)S(1)}, u32[]{:S(2)}, u32[]{:S(2)}) %collective-permute-start.2) | collective-permute-done | bytes 737312 | tf_op jit(solution)/shard_map/ppermute | solution.py:18
  247.9 0.4 copy.31
  248.4 21.4 %fusion.125 = bf16[24,32,1024]{2,1,0:T(8,128)(2,1)} fusion(bf16[24,15,1024]{2,1,0:T(8,128)(2,1)S(1)} %copy.32, bf16[24,32,1024]{2,1,0:T(8,128)(2,1)S(1)} %get-tuple-element.106, bf16[24,15,1024]{2,1,0:T(8,128)(2,1)S(1)} %copy.31, f32[]{:T(128)} %bitcast.62, f32[]{:T(128)} %bitcast.61, f32[]{:T(128)} %bitcast.60, f32[]{:T(128)} %bitcast.59, f32[]{:T(128)} %bitcast.58, ...), kind=kOutput, calls=%fused_computation.100 | convolution fusion | flops 107632768 | bytes 4620412 | tf_op jit(solution)/shard_map/zxy,xw->zwy/dot_general | solution.py:39
  269.7 26.7 %fusion.85 = f32[24,32,1024]{2,0,1:T(8,128)} fusion(bf16[24,24,1]{1,0,2:T(8,128)(2,1)S(1)} %fusion.233, f32[]{:T(128)} %bitcast.107, f32[]{:T(128)} %bitcast.106, f32[]{:T(128)} %bitcast.105, f32[]{:T(128)} %bitcast.104, f32[]{:T(128)} %bitcast.103, f32[]{:T(128)} %bitcast.102, f32[]{:T(128)} %bitcast.101, f32[]{:T(128)} %bitcast.100, f32[]{:T(128)} %bitcast.99, ...), kind=kOutput, calls=%fused_computation.85 | convolution fusion | flops 1748762624 | bytes 4719868 | tf_op jit(solution)/shard_map/zxy,wz->wxy/dot_general | solution.py:63
  296.5 138.8 %all-reduce.3.cloned.1.call-done = f32[24,32,1024]{2,0,1:T(8,128)} async-done(((f32[24,32,1024]{2,0,1:T(8,128)}), f32[24,32,1024]{2,0,1:T(8,128)}) %all-reduce.3.cloned.1.call-update) | async-done | bytes 3145744 | tf_op jit(solution)/shard_map/psum | solution.py:125
  435.3 3.8 fusion.131
  439.2 1.9 collective-permute-start.4
  441.2 4.0 collective-permute-start.5
  445.2 10.8 %collective-permute-done.4 = bf16[24,15,1024]{2,0,1:T(8,128)(2,1)S(1)} collective-permute-done((bf16[24,15,1024]{2,0,1:T(8,128)(2,1)S(1)}, bf16[24,15,1024]{2,0,1:T(8,128)(2,1)S(1)}, u32[]{:S(2)}, u32[]{:S(2)}) %collective-permute-start.4) | collective-permute-done | bytes 737312 | tf_op jit(solution)/shard_map/ppermute | solution.py:18
  456.0 1.4 collective-permute-done.5
  457.7 24.1 %fusion.119 = bf16[24,32,1024]{2,1,0:T(8,128)(2,1)} fusion(bf16[24,62,1024]{2,0,1:T(8,128)(2,1)S(1)} %pad_maximum_fusion, f32[]{:T(128)} %bitcast.62, f32[]{:T(128)} %bitcast.61, f32[]{:T(128)} %bitcast.60, f32[]{:T(128)} %bitcast.59, f32[]{:T(128)} %bitcast.58, f32[]{:T(128)} %bitcast.57, f32[]{:T(128)} %bitcast.56, f32[]{:T(128)} %bitcast.55, ...), kind=kOutput, calls=%fused_computation.98 | convolution fusion | flops 98490496 | bytes 4620412 | tf_op jit(solution)/shard_map/zxy,xw->zwy/dot_general | solution.py:39
  481.8 27.0 %fusion.91 = f32[24,32,1024]{2,0,1:T(8,128)} fusion(bf16[24,24,1]{1,0,2:T(8,128)(2,1)S(1)} %fusion.233, f32[]{:T(128)} %bitcast.107, f32[]{:T(128)} %bitcast.106, f32[]{:T(128)} %bitcast.105, f32[]{:T(128)} %bitcast.104, f32[]{:T(128)} %bitcast.103, f32[]{:T(128)} %bitcast.102, f32[]{:T(128)} %bitcast.101, f32[]{:T(128)} %bitcast.100, f32[]{:T(128)} %bitcast.99, ...), kind=kOutput, calls=%fused_computation.87 | convolution fusion | flops 1748762624 | bytes 4719868 | tf_op jit(solution)/shard_map/zxy,zw->wxy/dot_general | solution.py:51
  508.9 4.7 fusion.50
  513.9 0.4 copy.40
  514.3 3.8 collective-permute-start.7
  518.1 0.4 copy.39
  518.6 3.3 collective-permute-start.6
  521.8 7.6 %collective-permute-done.7 = bf16[24,15,1024]{2,0,1:T(8,128)(2,1)S(1)} collective-permute-done((bf16[24,15,1024]{2,0,1:T(8,128)(2,1)S(1)}, bf16[24,15,1024]{2,0,1:T(8,128)(2,1)S(1)}, u32[]{:S(2)}, u32[]{:S(2)}) %collective-permute-start.7) | collective-permute-done | bytes 737312 | tf_op jit(solution)/shard_map/ppermute | solution.py:20
  529.5 0.4 copy.42
  529.9 8.6 %collective-permute-done.6 = bf16[24,15,1024]{2,0,1:T(8,128)(2,1)S(1)} collective-permute-done((bf16[24,15,1024]{2,0,1:T(8,128)(2,1)S(1)}, bf16[24,15,1024]{2,0,1:T(8,128)(2,1)S(1)}, u32[]{:S(2)}, u32[]{:S(2)}) %collective-permute-start.6) | collective-permute-done | bytes 737312 | tf_op jit(solution)/shard_map/ppermute | solution.py:18
  538.4 0.4 copy.41
  538.9 21.4 %fusion.128 = bf16[24,32,1024]{2,1,0:T(8,128)(2,1)} fusion(bf16[24,15,1024]{2,1,0:T(8,128)(2,1)S(1)} %copy.42, bf16[24,32,1024]{2,1,0:T(8,128)(2,1)S(1)} %fusion.50, bf16[24,15,1024]{2,1,0:T(8,128)(2,1)S(1)} %copy.41, f32[]{:T(128)} %bitcast.62, f32[]{:T(128)} %bitcast.61, f32[]{:T(128)} %bitcast.60, f32[]{:T(128)} %bitcast.59, f32[]{:T(128)} %bitcast.58, ...), kind=kOutput, calls=%fused_computation.101 | convolution fusion | flops 107632768 | bytes 4620412 | tf_op jit(solution)/shard_map/zxy,xw->zwy/dot_general | solution.py:39
  560.2 26.7 %fusion.97 = f32[24,32,1024]{2,0,1:T(8,128)} fusion(bf16[24,24,1]{1,0,2:T(8,128)(2,1)S(1)} %fusion.233, f32[]{:T(128)} %bitcast.107, f32[]{:T(128)} %bitcast.106, f32[]{:T(128)} %bitcast.105, f32[]{:T(128)} %bitcast.104, f32[]{:T(128)} %bitcast.103, f32[]{:T(128)} %bitcast.102, f32[]{:T(128)} %bitcast.101, f32[]{:T(128)} %bitcast.100, f32[]{:T(128)} %bitcast.99, ...), kind=kOutput, calls=%fused_computation.89 | convolution fusion | flops 1748762624 | bytes 4719868 | tf_op jit(solution)/shard_map/zxy,wz->wxy/dot_general | solution.py:63
  587.0 132.1 %all-reduce.5.cloned.1.call-done = f32[24,32,1024]{2,0,1:T(8,128)} async-done(((f32[24,32,1024]{2,0,1:T(8,128)}), f32[24,32,1024]{2,0,1:T(8,128)}) %all-reduce.5.cloned.1.call-update) | async-done | bytes 3145744 | tf_op jit(solution)/shard_map/psum | solution.py:125
  719.1 5.6 multiply_multiply_fusion
  724.8 3.5 copy.44
  (24 shorter events, 2.3 us)
Async XLA Ops:
  11.1 38.7 %all-to-all-start.1 = ((s32[64,1,2]{2,1,0:T(1,128)}), s32[64,1,2]{2,1,0:T(1,128)S(1)}, u32[]{:S(2)}, u32[]{:S(2)}) async-start(s32[64,1,2]{2,1,0:T(1,128)} %bitcast.71), calls=%async_computation.1 | async-start | bytes 65536 | tf_op jit(solution)/shard_map/all_to_all | solution.py:91
  49.9 9.3 %copy-start = (f32[24,32,1024]{2,1,0:T(8,128)S(1)}, f32[24,32,1024]{2,1,0:T(8,128)}, u32[]{:S(2)}) copy-start(f32[24,32,1024]{2,1,0:T(8,128)} %param.9) | copy-start | bytes 9437188
  49.9 148.2 %all-to-all-start = ((bf16[64,2,24,1024]{3,1,2,0:T(2,128)(2,1)}), bf16[64,2,24,1024]{3,1,2,0:T(2,128)(2,1)}, u32[]{:S(2)}, u32[]{:S(2)}) async-start(bf16[64,2,24,1024]{3,1,2,0:T(2,128)(2,1)} %copy.19), calls=%async_computation | async-start | bytes 12582912 | tf_op jit(solution)/shard_map/all_to_all | solution.py:84
  59.1 376.3 %all-reduce.3.cloned.1.call-start = ((), (), s32[]{:S(2)}) async-start(), calls=%async_computation.2 | async-start | bytes 6291456 | tf_op jit(solution)/shard_map/psum | solution.py:125
  59.4 1.1 copy-start.1
  60.5 7.8 %copy-start.2 = (f32[1,3,31]{2,0,1:T(1,128)S(1)}, f32[1,3,31]{2,0,1:T(1,128)}, u32[]{:S(2)}) copy-start(f32[1,3,31]{2,0,1:T(1,128)} %param.8) | copy-start | bytes 1120
  62.2 82.9 %collective-permute-start.1 = (bf16[24,15,1024]{2,0,1:T(8,128)(2,1)}, bf16[24,15,1024]{2,0,1:T(8,128)(2,1)}, u32[]{:S(2)}, u32[]{:S(2)}) collective-permute-start(bf16[24,15,1024]{2,0,1:T(8,128)(2,1)} %copy.23), channel_id=1, source_target_pairs={{1,0},{2,1},{3,2},{4,3},{5,4},{6,5},{7,6},{8,7},{9,8},{10,9},{11,1... | collective-permute-start | bytes 2211848 | tf_op jit(solution)/shard_map/ppermute | solution.py:20
  65.7 80.9 %collective-permute-start = (bf16[24,15,1024]{2,0,1:T(8,128)(2,1)}, bf16[24,15,1024]{2,0,1:T(8,128)(2,1)}, u32[]{:S(2)}, u32[]{:S(2)}) collective-permute-start(bf16[24,15,1024]{2,0,1:T(8,128)(2,1)} %copy.22), channel_id=1, source_target_pairs={{0,1},{1,2},{2,3},{3,4},{4,5},{5,6},{6,7},{7,8},{8,9},{9,10},{10,1... | collective-permute-start | bytes 2211848 | tf_op jit(solution)/shard_map/ppermute | solution.py:18
  224.7 15.3 %collective-permute-start.3 = (bf16[24,15,1024]{2,0,1:T(8,128)(2,1)S(1)}, bf16[24,15,1024]{2,0,1:T(8,128)(2,1)S(1)}, u32[]{:S(2)}, u32[]{:S(2)}) collective-permute-start(bf16[24,15,1024]{2,0,1:T(8,128)(2,1)S(1)} %copy.30), channel_id=1, source_target_pairs={{1,0},{2,1},{3,2},{4,3},{5,4},{6,5},{7,6},{8,7},{9,8},{10,9},{11,1... | collective-permute-start | bytes 2211848 | tf_op jit(solution)/shard_map/ppermute | solution.py:20
  228.9 19.0 %collective-permute-start.2 = (bf16[24,15,1024]{2,0,1:T(8,128)(2,1)S(1)}, bf16[24,15,1024]{2,0,1:T(8,128)(2,1)S(1)}, u32[]{:S(2)}, u32[]{:S(2)}) collective-permute-start(bf16[24,15,1024]{2,0,1:T(8,128)(2,1)S(1)} %copy.29), channel_id=1, source_target_pairs={{0,1},{1,2},{2,3},{3,4},{4,5},{5,6},{6,7},{7,8},{8,9},{9,10},{10,1... | collective-permute-start | bytes 2211848 | tf_op jit(solution)/shard_map/ppermute | solution.py:18
  296.5 422.6 %all-reduce.5.cloned.1.call-start = ((), (), s32[]{:S(2)}) async-start(), calls=%async_computation.3 | async-start | bytes 6291456 | tf_op jit(solution)/shard_map/psum | solution.py:125
  439.2 16.7 %collective-permute-start.4 = (bf16[24,15,1024]{2,0,1:T(8,128)(2,1)S(1)}, bf16[24,15,1024]{2,0,1:T(8,128)(2,1)S(1)}, u32[]{:S(2)}, u32[]{:S(2)}) collective-permute-start(bf16[24,15,1024]{2,0,1:T(8,128)(2,1)S(1)} %get-tuple-element.7), channel_id=1, source_target_pairs={{0,1},{1,2},{2,3},{3,4},{4,5},{5,6},{6,7},{7,8},{8,9},{9,10},{10,1... | collective-permute-start | bytes 2211848 | tf_op jit(solution)/shard_map/ppermute | solution.py:18
  441.2 16.2 %collective-permute-start.5 = (bf16[24,15,1024]{2,0,1:T(8,128)(2,1)S(1)}, bf16[24,15,1024]{2,0,1:T(8,128)(2,1)S(1)}, u32[]{:S(2)}, u32[]{:S(2)}) collective-permute-start(bf16[24,15,1024]{2,0,1:T(8,128)(2,1)S(1)} %get-tuple-element.8), channel_id=1, source_target_pairs={{1,0},{2,1},{3,2},{4,3},{5,4},{6,5},{7,6},{8,7},{9,8},{10,9},{11,1... | collective-permute-start | bytes 2211848 | tf_op jit(solution)/shard_map/ppermute | solution.py:20
  514.3 15.1 %collective-permute-start.7 = (bf16[24,15,1024]{2,0,1:T(8,128)(2,1)S(1)}, bf16[24,15,1024]{2,0,1:T(8,128)(2,1)S(1)}, u32[]{:S(2)}, u32[]{:S(2)}) collective-permute-start(bf16[24,15,1024]{2,0,1:T(8,128)(2,1)S(1)} %copy.40), channel_id=1, source_target_pairs={{1,0},{2,1},{3,2},{4,3},{5,4},{6,5},{7,6},{8,7},{9,8},{10,9},{11,1... | collective-permute-start | bytes 2211848 | tf_op jit(solution)/shard_map/ppermute | solution.py:20
  518.6 19.9 %collective-permute-start.6 = (bf16[24,15,1024]{2,0,1:T(8,128)(2,1)S(1)}, bf16[24,15,1024]{2,0,1:T(8,128)(2,1)S(1)}, u32[]{:S(2)}, u32[]{:S(2)}) collective-permute-start(bf16[24,15,1024]{2,0,1:T(8,128)(2,1)S(1)} %copy.39), channel_id=1, source_target_pairs={{0,1},{1,2},{2,3},{3,4},{4,5},{5,6},{6,7},{7,8},{8,9},{9,10},{10,1... | collective-permute-start | bytes 2211848 | tf_op jit(solution)/shard_map/ppermute | solution.py:18
Sparse Core Ops, SparseCore 0:
  296.6 138.6 all-reduce.2
  587.1 131.9 all-reduce.4
where the time goes:
time: 745 us; the launch traced here: 735 us
  waiting for transfers between devices  367 us (49%)
  matrix products  206 us (28%)
  local copies, waits for them, and re-layouts  67.6 us (9%)
  starting transfers between devices  42.7 us (6%)
  other arithmetic  38.2 us (5%)
  between operations  13.9 us (2%)
    psum x2, waiting for transfers between devices, per_device(): summed_views = lax.psum(partial_value, 'view')  271 us
    dot_general x4, matrix products, across_columns(): jnp.einsum('zxy,xw->zwy', field.astype(jnp.bfloat16), matrix, preferred_e...  89.7 us
    ppermute x4, waiting for transfers between devices, padded(): lax.ppermute(head, axis, [((i + 1) % count, i) for i in range(ends)])  69 us
    dot_general x2, matrix products, across_depth(): jnp.einsum('zxy,zw->wxy', field.astype(jnp.bfloat16), matrix, preferred_e...  54.1 us
    dot_general x2, matrix products, mirror_depth(): jnp.einsum('zxy,wz->wxy', field.astype(jnp.bfloat16), matrix, preferred_e...  53.4 us
    ppermute x4, waiting for transfers between devices, padded(): lax.ppermute(tail, axis, [(i, (i + 1) % count) for i in range(ends)])  26.9 us
    convert_element_type x1, other arithmetic, banded(): return matrix.astype(jnp.bfloat16)  19.4 us
  transfers between devices with their start and end apart: 12, of which 9 were waited for; matrix products, arithmetic and copies ran while one was open for 15% of the time, Pallas kernels for 0%

commit v1 on v0

v1 whole, which is shorter than its diff:
```python
import functools

import jax
import jax.numpy as jnp
import numpy as np
from jax import lax
from jax.experimental import pallas as pl
from jax.experimental.pallas import tpu as pltpu
from jax.sharding import PartitionSpec as P

ITERS = 2
TAPS = 31
HALF = 15
VIEWS = 4
NZ = 24
BX = 32
MARGIN = 16
EX = BX + 2 * MARGIN
YQ = 256
YE = 384
TURN = 320
ROWS = BX * NZ
ZI = 8
ZG = NZ // ZI
XR = BX * ZI
EXR = EX * ZI
GX = 8
GR = GX * ZI
ZR = GX * NZ
FULL = 32700.0
STEPS = 128.0
LN2 = float(np.log(2.0))
M_MID, M_SCALE = 2.125, 32767.0 / 1.875
E_SCALE = 32767.0 / 2.0
VMEM = 56 * 1024 * 1024

f32, bf16, i32, i16 = jnp.float32, jnp.bfloat16, jnp.int32, jnp.int16


def params():
    return pltpu.CompilerParams(vmem_limit_bytes=VMEM)


def cost(flops, moved):
    return pl.CostEstimate(flops=int(flops), bytes_accessed=int(moved), transcendentals=0)


def dot(a, b):
    return jnp.dot(a, b, preferred_element_type=f32)


def halves(x):
    hi = x.astype(bf16)
    return hi, (x - hi.astype(f32)).astype(bf16)


def to_code(x):
    return jnp.floor(x + 0.5).astype(i32).astype(i16)


def from_code(c):
    return c.astype(i32).astype(f32)


def scale_steps(top):
    return jnp.ceil(jnp.log(jnp.maximum(top, 1e-30)) * (STEPS / LN2))


def lane_code(value):
    k = scale_steps(jnp.max(jnp.abs(value), axis=0, keepdims=True))
    code = to_code(value * (jnp.exp(k * (-LN2 / STEPS)) * FULL))
    return code, jnp.broadcast_to(k, (16, value.shape[1])).astype(i32).astype(i16)


def lane_value(ref):
    n = ref.shape[0] - 16
    k = from_code(ref[n:])[0:1]
    return from_code(ref[:n]) * (jnp.exp(k * (LN2 / STEPS)) * (1.0 / FULL))


def send(ref, value):
    n = value.shape[0]
    ref[:n], ref[n:] = lane_code(value)


def flat(x):
    return x.reshape(x.shape[0] * x.shape[1], x.shape[2])


LOADS = 4
SLOT = NZ * 8


def pack_body(cap, blocks, columns, tiles, out, labels, count, slots, held, sent, loaded, sem):
    pieces = tiles.shape[0]
    part = pieces // LOADS
    groups = out.shape[0]

    def load(i):
        rows = pl.ds(i * part, part)
        return pltpu.make_async_copy(tiles.at[rows], held.at[rows], loaded.at[i])

    for i in range(LOADS):
        load(i).start()

    def clear(i, _):
        labels[i] = 0
        return 0

    lax.fori_loop(0, groups * cap, clear, 0)

    def zero(i, _):
        count[i] = 0
        return 0

    lax.fori_loop(0, groups, zero, 0)

    def route(p, _):
        b = blocks[p]
        rank = count[b]
        count[b] = rank + 1
        slot = b * cap + rank
        labels[slot] = columns[p] + 1
        slots[p] = slot
        return 0

    lax.fori_loop(0, pieces, route, 0)
    lane = lax.broadcasted_iota(i32, (16, 128), 1)

    def mark(b, _):
        row = jnp.zeros((16, 128), i32)
        for rank in range(cap):
            row = jnp.where(lane == rank, labels[b * cap + rank], row)
        sent[b, cap * SLOT :, :] = row.astype(f32).astype(bf16)
        return 0

    lax.fori_loop(0, groups, mark, 0)
    for i in range(LOADS):
        load(i).wait()

        def put(p, _):
            slot = slots[p]
            b = slot // cap
            at = (slot - b * cap) * SLOT
            for c in range(8):
                rows = pl.ds(pl.multiple_of(at + 16 * c, 16), 16)
                sent[b, rows, :] = held[p, :16, 128 * c : 128 * (c + 1)]
            for c in range(0, 8, 2):
                rows = pl.ds(pl.multiple_of(at + 128 + 8 * c, 16), 16)
                sent[b, rows, :] = jnp.concatenate(
                    [
                        held[p, 16:, 128 * c : 128 * (c + 1)],
                        held[p, 16:, 128 * (c + 1) : 128 * (c + 2)],
                    ],
                    axis=0,
                )
            return 0

        lax.fori_loop(i * part, (i + 1) * part, put, 0, unroll=2)
    push = pltpu.make_async_copy(sent, out, sem)
    push.start()
    push.wait()


def pack(cap, groups, blocks, columns, tiles):
    smem = pl.BlockSpec(memory_space=pltpu.SMEM)
    message = (groups, cap * SLOT + 16, 128)
    return pl.pallas_call(
        functools.partial(pack_body, cap),
        out_shape=jax.ShapeDtypeStruct(message, bf16),
        in_specs=[smem, smem, pl.BlockSpec(memory_space=pl.ANY)],
        out_specs=pl.BlockSpec(memory_space=pl.ANY),
        scratch_shapes=[
            pltpu.SMEM((groups * cap,), i32),
            pltpu.SMEM((groups,), i32),
            pltpu.SMEM((tiles.shape[0],), i32),
            pltpu.VMEM(tiles.shape, bf16),
            pltpu.VMEM(message, bf16),
            pltpu.SemaphoreType.DMA((LOADS,)),
            pltpu.SemaphoreType.DMA,
        ],
        compiler_params=params(),
        cost_estimate=cost(0, 4 * tiles.size),
    )(blocks, columns, tiles)


def unpack_body(cap, chunk, place, arrived, whole_arrived, *rest):
    outs, (acc, count, marks, table, labels, sem) = rest[:VIEWS], rest[VIEWS:]
    step = pl.program_id(0)
    layer = place[1]

    @pl.when(step == 0)
    def _():
        fetch = pltpu.make_async_copy(
            whole_arrived.at[:, pl.ds(cap * SLOT, 16), :], marks, sem.at[0]
        )
        fetch.start()
        acc[...] = jnp.zeros_like(acc)

        def zero(i, _):
            count[i] = 0
            return 0

        lax.fori_loop(0, BX, zero, 0)
        fetch.wait()
        table[...] = jnp.max(marks[...].astype(f32), axis=1).astype(i32)
        move = pltpu.make_async_copy(table, labels, sem.at[1])
        move.start()
        move.wait()

    for j in range(chunk):
        for rank in range(cap):
            label = labels[step * chunk + j, rank]

            @pl.when(label > 0)
            def _():
                col = label - 1
                rows = pl.ds(pl.multiple_of(col * ZI, ZI), ZI)
                tile = arrived[j, rank * SLOT : (rank + 1) * SLOT, :].astype(f32)
                for c in range(8):
                    lanes = slice(128 * c, 128 * (c + 1))
                    acc[0, rows, lanes] += tile[16 * c : 16 * c + 8]
                    acc[1, rows, lanes] += tile[16 * c + 8 : 16 * c + 16]
                    acc[2, rows, lanes] += tile[128 + 8 * c : 136 + 8 * c]
                count[col] += 1

    @pl.when(step == pl.num_programs(0) - 1)
    def _():
        row = lax.broadcasted_iota(i32, (2 * ZI, 128), 0)
        lane = lax.broadcasted_iota(i32, (2 * ZI, 128), 1)

        def pair(i, _):
            first = M_SCALE / jnp.maximum(count[2 * i], 1).astype(f32)
            second = M_SCALE / jnp.maximum(count[2 * i + 1], 1).astype(f32)
            inverse = jnp.where(row < ZI, first, second)
            for g in range(ZG):
                rows = pl.ds(pl.multiple_of(i * 2 * ZI, 2 * ZI), 2 * ZI)
                to = pl.ds(pl.multiple_of(g * XR + i * 2 * ZI, 2 * ZI), 2 * ZI)

                def code_at(lane_block):
                    lanes = pl.ds(pl.multiple_of(lane_block * 128, 128), 128)
                    code = acc[g, rows, lanes] * inverse - M_MID * M_SCALE
                    return jnp.clip(code, -32767.0, 32767.0)

                for r in range(VIEWS):
                    base = 2 * lax.rem(layer + r, VIEWS)
                    after = code_at(jnp.minimum(base + 2, 2 * VIEWS - 1))
                    before = code_at(jnp.maximum(base - 1, 0))
                    outs[r][to, 0:128] = to_code(code_at(base))
                    outs[r][to, 128:256] = to_code(code_at(base + 1))
                    outs[r][to, 256:384] = to_code(jnp.where(lane < 64, after, before))
            return 0

        lax.fori_loop(0, BX // 2, pair, 0)


def unpack(cap, place, arrived):
    groups = arrived.shape[0]
    chunk = min(8, groups)
    smem = pl.BlockSpec(memory_space=pltpu.SMEM)
    return pl.pallas_call(
        functools.partial(unpack_body, cap, chunk),
        grid=(groups // chunk,),
        out_shape=(jax.ShapeDtypeStruct((ROWS, YE), i16),) * VIEWS,
        in_specs=[
            smem,
            pl.BlockSpec((chunk,) + arrived.shape[1:], lambda s: (s, 0, 0)),
            pl.BlockSpec(memory_space=pl.ANY),
        ],
        out_specs=(pl.BlockSpec((ROWS, YE), lambda s: (0, 0)),) * VIEWS,
        scratch_shapes=[
            pltpu.VMEM((ZG, XR, VIEWS * YQ), f32),
            pltpu.SMEM((BX,), i32),
            pltpu.VMEM((groups, 16, 128), bf16),
            pltpu.VMEM((groups, 128), i32),
            pltpu.SMEM((groups, 128), i32),
            pltpu.SemaphoreType.DMA((2,)),
        ],
        compiler_params=params(),
        cost_estimate=cost(arrived.size, 2 * arrived.size),
    )(place, arrived, arrived)


def iota(shape, dim):
    return lax.broadcasted_iota(i32, shape, dim)


def bands_body(taps, kx, kxt, ty, tyt, bz, bzt):
    r = pl.program_id(0)

    def band(distance, axis):
        out = jnp.zeros(distance.shape, f32)
        for t in range(TAPS):
            out = jnp.where(distance == t, taps[r, axis * TAPS + t], out)
        return out

    def kept(x):
        return lax.shift_right_logical(x, 3)

    def inner(x):
        return lax.bitwise_and(x, ZI - 1)

    row, col = iota((XR, EXR), 0), iota((XR, EXR), 1)
    same = inner(row) == inner(col)
    kx[0] = jnp.where(same, band(kept(col) - kept(row) - 1, 1), 0.0).astype(bf16)
    row, col = iota((EXR, XR), 0), iota((EXR, XR), 1)
    same = inner(row) == inner(col)
    kxt[0] = jnp.where(same, band(kept(row) - kept(col) - 1, 1), 0.0).astype(bf16)

    def place(k):
        return jnp.where(k < TURN, k, k - YE)

    apart = place(iota((YE, YE), 0)) - place(iota((YE, YE), 1))
    ty[0] = band(apart + HALF, 2).astype(bf16)
    back = band(HALF - apart, 2).astype(bf16)
    tyt[0, :YE] = back
    tyt[0, YE:] = back

    def parts(x):
        group = jnp.where(x >= 2 * GR, 2, jnp.where(x >= GR, 1, 0))
        within = x - group * GR
        return group * ZI + inner(within), kept(within)

    (zr, xr), (zc, xc) = parts(iota((ZR, ZR), 0)), parts(iota((ZR, ZR), 1))
    bz[0] = jnp.where(xr == xc, band(zc - zr + HALF, 0), 0.0).astype(bf16)
    (zr, xr), col = parts(iota((ZR, 2 * ZR), 0)), iota((ZR, 2 * ZR), 1)
    zc, xc = parts(jnp.where(col >= ZR, col - ZR, col))
    bzt[0] = jnp.where(xr == xc, band(zr - zc + HALF, 0), 0.0).astype(bf16)


MATS = [(XR, EXR), (EXR, XR), (YE, YE), (2 * YE, YE), (ZR, ZR), (ZR, 2 * ZR)]


def bands(taps):
    return pl.pallas_call(
        bands_body,
        grid=(VIEWS,),
        out_shape=tuple(jax.ShapeDtypeStruct((VIEWS,) + s, bf16) for s in MATS),
        in_specs=[pl.BlockSpec(memory_space=pltpu.SMEM)],
        out_specs=tuple(pl.BlockSpec((1,) + s, lambda r: (r, 0, 0)) for s in MATS),
        compiler_params=params(),
        cost_estimate=cost(4e9, 2e7),
    )(taps)


def cell_body(place, start, own, left, right, scratch):
    layer = place[1]
    last = start.shape[2] - 128
    after = jnp.minimum((layer + 1) * YQ, last)
    before = jnp.maximum(layer * YQ - 128, 0)
    lane = iota((BX, 128), 1)
    for z in range(NZ):
        rows = pl.ds(z // ZI * XR + z % ZI, BX, stride=ZI)
        for c in range(2):
            at = pl.multiple_of(layer * YQ + c * 128, 128)
            scratch[c, rows, :] = start[z, :, pl.ds(at, 128)]
        head = start[z, :, pl.ds(pl.multiple_of(after, 128), 128)]
        tail = start[z, :, pl.ds(pl.multiple_of(before, 128), 128)]
        head = jnp.where((lane < TURN - YQ) & (layer < VIEWS - 1), head, 0.0)
        tail = jnp.where((lane >= TURN - YQ) & (layer > 0), tail, 0.0)
        scratch[2, rows, :] = head + tail
    value = jnp.concatenate([scratch[c] for c in range(3)], axis=1)
    own[...] = value.reshape(ZG, XR, YE)
    code = to_code(value * E_SCALE).reshape(ZG, XR, YE)
    left[...] = code[:, : XR // 2]
    right[...] = code[:, XR // 2 :]


def cell(place, start):
    half = jax.ShapeDtypeStruct((ZG, XR // 2, YE), i16)
    return pl.pallas_call(
        cell_body,
        out_shape=(jax.ShapeDtypeStruct((ZG, XR, YE), f32), half, half),
        in_specs=[
            pl.BlockSpec(memory_space=pltpu.SMEM),
            pl.BlockSpec(memory_space=pltpu.VMEM),
        ],
        scratch_shapes=[pltpu.VMEM((3, ROWS, 128), f32)],
        compiler_params=params(),
        cost_estimate=cost(3e6, 6e6),
    )(place, start)


def blurred(field, kx, ty, bz):
    x = jnp.concatenate([dot(kx, field[g]).astype(bf16) for g in range(ZG)], axis=0)
    y = dot(x, ty).astype(bf16)
    return [dot(bz, columns_of(y, XR, c)) for c in range(BX // GX)]


def columns_of(rows, stride, c):
    return jnp.concatenate(
        [rows[g * stride + c * GR : g * stride + (c + 1) * GR] for g in range(ZG)], axis=0
    )


def rows_from(groups):
    return jnp.concatenate(
        [part[g * GR : (g + 1) * GR] for g in range(ZG) for part in groups], axis=0
    )


def mirrored(quotient, kxt, tyt, bzt, pairs):
    parts = [halves(dot(kxt, quotient[g * XR : (g + 1) * XR])) for g in range(ZG)]
    hi = jnp.concatenate([p[0] for p in parts], axis=0)
    lo = jnp.concatenate([p[1] for p in parts], axis=0)
    for c in range(EX // GX):
        both = jnp.concatenate([columns_of(hi, EXR, c), columns_of(lo, EXR, c)], axis=0)
        z_hi, z_lo = halves(dot(bzt, both))
        for g in range(ZG):
            rows = slice(g * EXR + c * GR, g * EXR + (c + 1) * GR)
            pairs[rows, :YE] = z_hi[g * GR : (g + 1) * GR]
            pairs[rows, YE:] = z_lo[g * GR : (g + 1) * GR]
    return dot(pairs[...], tyt)


def quotient_of(layer, code, blur_now):
    lane = iota(code.shape, 1)
    inside = (lane < YQ) | ((lane < TURN) & (layer < VIEWS - 1)) | ((lane >= TURN) & (layer > 0))
    measured = jnp.where(inside, from_code(code) * (1.0 / M_SCALE) + M_MID, 0.0)
    return (measured / jnp.where(inside, blur_now, 1.0)).astype(bf16)


def widened(own, from_left, from_right):
    inverse = 1.0 / E_SCALE
    return jnp.concatenate(
        [from_code(from_left) * inverse, own, from_code(from_right) * inverse], axis=1
    )


def mat_spec(n, at=None):
    index = (lambda r: (r, 0, 0)) if at is None else (lambda *_: (at, 0, 0))
    return pl.BlockSpec((1,) + MATS[n], index)


def whole(shape):
    return pl.BlockSpec(shape, lambda *_: (0,) * len(shape))


def blur_body(own, from_left, from_right, kx, ty, bz, out, field):
    @pl.when(pl.program_id(0) == 0)
    def _():
        field[...] = widened(own[...], from_left[...], from_right[...]).astype(bf16)

    out[0] = rows_from(blurred(field, kx[0], ty[0], bz[0]))


def blur(own, from_left, from_right, mats):
    return pl.pallas_call(
        blur_body,
        grid=(VIEWS,),
        out_shape=jax.ShapeDtypeStruct((VIEWS, ROWS, YE), f32),
        in_specs=[
            whole(own.shape),
            whole(from_left.shape),
            whole(from_right.shape),
            mat_spec(0),
            mat_spec(2),
            mat_spec(4),
        ],
        out_specs=pl.BlockSpec((1, ROWS, YE), lambda r: (r, 0, 0)),
        scratch_shapes=[pltpu.VMEM((ZG, EXR, YE), bf16)],
        compiler_params=params(),
        cost_estimate=cost(7e9, 1.6e7),
    )(own, from_left, from_right, mats[0], mats[2], mats[4])


def mirror_body(first, last, place, code, blur_ref, kxt, tyt, bzt, *rest):
    rest, pairs = list(rest[:-1]), rest[-1]
    before = None if first else rest.pop(0)
    total = rest.pop(0)
    quotient = quotient_of(place[1], code[...], blur_ref[0])
    value = mirrored(quotient, kxt[0], tyt[0], bzt[0], pairs).reshape(ZG, EXR, YE)
    if not first:
        value = value + before[...]
    total[...] = value
    if last:
        left, right = rest
        send(left, flat(value[:, : EXR // 2]))
        send(right, flat(value[:, EXR // 2 :]))


def mirror(r, place, code, blur_all, mats, before):
    first, last = r == 0, r == VIEWS - 1
    columns = jax.ShapeDtypeStruct((ZG * EXR // 2 + 16, YE), i16)
    shapes = [jax.ShapeDtypeStruct((ZG, EXR, YE), f32)] + [columns, columns] * last
    operands = [place, code, blur_all, mats[1], mats[3], mats[5]] + [before] * (not first)
    return pl.pallas_call(
        functools.partial(mirror_body, first, last),
        grid=(1,),
        out_shape=tuple(shapes),
        in_specs=[
            pl.BlockSpec(memory_space=pltpu.SMEM),
            whole(code.shape),
            pl.BlockSpec((1, ROWS, YE), lambda *_: (r, 0, 0)),
            mat_spec(1, r),
            mat_spec(3, r),
            mat_spec(5, r),
        ]
        + [whole((ZG, EXR, YE))] * (not first),
        out_specs=tuple(whole(s.shape) for s in shapes),
        scratch_shapes=[pltpu.VMEM((ZG * EXR, 2 * YE), bf16)],
        compiler_params=params(),
        cost_estimate=cost(2e9, 8e6),
    )(*operands)


def second_body(place, own, e_left, e_right, total, x_left, x_right, *rest):
    codes = rest[:VIEWS]
    kx, kxt, ty, tyt, bz, bzt = rest[VIEWS : VIEWS + 6]
    estimate, center, left, right, field, acc, pairs = rest[VIEWS + 6 :]
    step = pl.program_id(0)
    edge = MARGIN * ZI
    middle = EXR // 2

    @pl.when(step == 0)
    def _():
        start = widened(own[...], e_left[...], e_right[...]) * (1.0 / VIEWS)
        for half, came in enumerate((x_left, x_right)):
            rows = slice(half * middle, (half + 1) * middle)
            now = start[:, rows] * (total[:, rows] + lane_value(came).reshape(ZG, middle, YE))
            field[:, rows] = now.astype(bf16)
            inner = now[:, edge:] if half == 0 else now[:, : middle - edge]
            estimate[:, half * edge : (half + 1) * edge] = inner[:, :, :YQ]
        acc[...] = jnp.zeros_like(acc)

    code = codes[0][...].astype(i32)
    for r in range(1, VIEWS):
        code = jnp.where(step == r, codes[r][...].astype(i32), code)
    blur_now = rows_from(blurred(field, kx[0], ty[0], bz[0]))
    quotient = quotient_of(place[1], code, blur_now)
    acc[...] += mirrored(quotient, kxt[0], tyt[0], bzt[0], pairs).reshape(ZG, EXR, YE)

    @pl.when(step == pl.num_programs(0) - 1)
    def _():
        center[...] = acc[:, edge : edge + XR, :YQ]
        send(left, flat(acc[:, :edge, :YQ]))
        send(right, flat(acc[:, edge + XR :, :YQ]))


def second(place, own, e_left, e_right, total, x_left, x_right, codes, mats):
    columns = jax.ShapeDtypeStruct((ZG * MARGIN * ZI + 16, YQ), i16)
    cell_shape = jax.ShapeDtypeStruct((ZG, XR, YQ), f32)
    shapes = (cell_shape, cell_shape, columns, columns)
    operands = (own, e_left, e_right, total, x_left, x_right) + tuple(codes)
    return pl.pallas_call(
        second_body,
        grid=(VIEWS,),
        out_shape=shapes,
        in_specs=[pl.BlockSpec(memory_space=pltpu.SMEM)]
        + [whole(a.shape) for a in operands]
        + [mat_spec(n) for n in range(6)],
        out_specs=tuple(whole(s.shape) for s in shapes),
        scratch_shapes=[
            pltpu.VMEM((ZG, EXR, YE), bf16),
            pltpu.VMEM((ZG, EXR, YE), f32),
            pltpu.VMEM((ZG * EXR, 2 * YE), bf16),
        ],
        compiler_params=params(),
        cost_estimate=cost(1.6e10, 4e7),
    )(place, *operands, *mats)


def finish_body(estimate, total, x_left, x_right, out):
    middle = XR // 2
    low = total[:, :middle] + lane_value(x_left).reshape(ZG, middle, YQ)
    high = total[:, middle:] + lane_value(x_right).reshape(ZG, middle, YQ)
    summed = jnp.concatenate([low, high], axis=1)
    send(out, flat(estimate[...] * summed * (1.0 / VIEWS)))


def finish(estimate, total, x_left, x_right):
    return pl.pallas_call(
        finish_body,
        out_shape=jax.ShapeDtypeStruct((ROWS + 16, YQ), i16),
        compiler_params=params(),
        cost_estimate=cost(5e6, 4e6),
    )(estimate, total, x_left, x_right)


def gather_body(place, *rest):
    codes, out, scratch = rest[:VIEWS], rest[VIEWS], rest[VIEWS + 1]
    layer = place[1]
    for r in range(VIEWS):
        value = lane_value(codes[r])
        at = lax.rem(layer + VIEWS - r, VIEWS) * YQ
        for c in range(2):
            scratch[r, c] = value[:, c * 128 : (c + 1) * 128]
            lanes = pl.ds(pl.multiple_of(at + c * 128, 128), 128)
            for z in range(NZ):
                rows = pl.ds(z // ZI * XR + z % ZI, BX, stride=ZI)
                out[z, :, lanes] = scratch[r, c, rows, :]


def gathered(place, codes):
    return pl.pallas_call(
        gather_body,
        out_shape=jax.ShapeDtypeStruct((NZ, BX, VIEWS * YQ), f32),
        in_specs=[pl.BlockSpec(memory_space=pltpu.SMEM)]
        + [pl.BlockSpec(memory_space=pltpu.VMEM)] * VIEWS,
        scratch_shapes=[pltpu.VMEM((VIEWS, 2, ROWS, 128), f32)],
        compiler_params=params(),
        cost_estimate=cost(3e6, 6e6),
    )(place, *codes)


def per_device(view_tiles, route_block, route_column, psf_taps, start_estimate):
    groups = lax.axis_size("block")
    cap = max(2, (2 * BX + groups - 1) // groups)
    me, layer = lax.axis_index("block"), lax.axis_index("view")
    place = jnp.stack([me, layer]).astype(i32)

    def around(x, shift):
        return lax.ppermute(x, "view", [(i, (i + shift) % VIEWS) for i in range(VIEWS)])

    def shifted(x, shift):
        pairs = [(i, i + shift) for i in range(groups) if 0 <= i + shift < groups]
        return lax.ppermute(x, "block", pairs)

    kernel = psf_taps[0] / jnp.sum(psf_taps[0], axis=1, keepdims=True)
    kernel = kernel.astype(bf16).astype(f32)
    taps = jnp.stack([kernel] + [around(kernel, r) for r in range(1, VIEWS)])

    outgoing = pack(cap, groups, route_block[0], route_column[0], view_tiles[0])
    outgoing, taps = lax.optimization_barrier((outgoing, taps))
    arrived = lax.all_to_all(outgoing, "block", split_axis=0, concat_axis=0, tiled=True)

    mats = bands(taps.reshape(VIEWS, 3 * TAPS))
    start_estimate, _ = lax.optimization_barrier((start_estimate, outgoing))
    own, to_left, to_right = cell(place, start_estimate)
    e_left, e_right = shifted(to_right, 1), shifted(to_left, -1)

    codes = unpack(cap, place, arrived)
    own, codes = lax.optimization_barrier((own, codes))
    codes = [codes[0]] + [around(codes[r], r) for r in range(1, VIEWS)]
    blur_all = blur(own, e_left, e_right, mats)
    parts = [None]
    for r in range(VIEWS):
        parts = mirror(r, place, codes[r], blur_all, mats, parts[0])
    total, left, right = parts
    x_left, x_right = shifted(right, 1), shifted(left, -1)
    estimate, center, left, right = second(
        place, own, e_left, e_right, total, x_left, x_right, codes, mats
    )
    x_left, x_right = shifted(right, 1), shifted(left, -1)
    final = finish(estimate, center, x_left, x_right)
    return gathered(place, [final] + [around(final, r) for r in range(1, VIEWS)])


def solution(mesh):
    placed = (
        P("view", "block", None, None),
        P("view", "block"),
        P("view", "block"),
        P("view", None, None),
        P(None, "block", None),
    )
    return jax.shard_map(
        per_device, mesh=mesh, in_specs=placed, out_specs=P(None, "block", None), check_vma=False
    )
```

time: 745 us -> 307 us (0.41); the launches traced: 735 us -> 306 us
  waiting for transfers between devices: 367 us -> 140 us
  matrix products: 206 us -> 0 us
  Pallas kernels: 0 us -> 110 us
  local copies, waits for them, and re-layouts: 67.6 us -> 6.51 us
  other arithmetic: 38.2 us -> 2.94 us
  between operations: 13.9 us -> 0.16 us
    psum x2 -> x0, waiting for transfers between devices: 271 us -> none  [per_device(): summed_views = lax.psum(partial_value, 'view')]
    dot_general x9 -> x0, matrix products: 206 us -> none  [the longest x4 89.7 us: across_columns(): jnp.einsum('zxy,xw->zwy', field.astype(jnp.bfloat16), matrix, preferred_e...]
    pallas_call x0 -> x12, Pallas kernels: none -> 110 us  [the longest x4 26.6 us: mirror(): pl.pallas_call(functools.partial(mirror_body, first, last), grid=(1,), ou...]
    all_to_all x2 -> x1, waiting for transfers between devices: 0.01 us -> 55.7 us  [per_device(): lax.all_to_all(outgoing, 'block', split_axis=0, concat_axis=0, tiled=True)]
    convert_element_type x5 -> x2, other arithmetic: 28.9 us -> 1.5 us  [per_device(): kernel = kernel.astype(bf16).astype(f32)]
    reshape x2 -> x1, local copies, waits for them, and re-layouts: 22.8 us -> 0.67 us  [per_device(): mats = bands(taps.reshape(VIEWS, 3 * TAPS))]
    scatter x2 -> x0, local copies, waits for them, and re-layouts: 14.5 us -> none  [the longest x1 13.7 us: per_device(): jnp.zeros((groups * capacity, depth, rows_y), jnp.bfloat16).at[slot_of]]
    ppermute x8 -> x15, starting transfers between devices: 24.6 us -> 38 us  [the longest x9 21.3 us: around(): lax.ppermute(x, 'view', [(i, (i + shift) % VIEWS) for i in range(VIEWS)])]
  transfers between devices with their start and end apart: 12 -> 16, of which waited for: 9 -> 8; matrix products, arithmetic and copies ran while one was open for 15% -> 1% of each run, Pallas kernels for 0% -> 24%
where the time goes in v1:
time: 307 us; the launch traced here: 306 us
  waiting for transfers between devices  140 us (46%)
  Pallas kernels  110 us (36%)
  starting transfers between devices  47 us (15%)
  local copies, waits for them, and re-layouts  6.51 us (2%)
    ppermute x9, waiting for transfers between devices, around(): lax.ppermute(x, 'view', [(i, (i + shift) % VIEWS) for i in range(VIEWS)])  68.3 us
    all_to_all x1, waiting for transfers between devices, per_device(): lax.all_to_all(outgoing, 'block', split_axis=0, concat_axis=0, tiled=True)  55.7 us
    pallas_call x4, Pallas kernels, mirror(): pl.pallas_call(functools.partial(mirror_body, first, last), grid=(1,), ou...  26.6 us
    pallas_call x1, Pallas kernels, bands(): pl.pallas_call(bands_body, grid=(VIEWS,), out_shape=tuple((jax.ShapeDtype...  22.6 us
    pallas_call x1, Pallas kernels, second(): pl.pallas_call(second_body, grid=(VIEWS,), out_shape=shapes, in_specs=[pl...  22.3 us
    ppermute x9, starting transfers between devices, around(): lax.ppermute(x, 'view', [(i, (i + shift) % VIEWS) for i in range(VIEWS)])  21.3 us
    ppermute x6, starting transfers between devices, shifted(): return lax.ppermute(x, 'block', pairs)  16.7 us
    ppermute x6, waiting for transfers between devices, shifted(): return lax.ppermute(x, 'block', pairs)  15.9 us
  transfers between devices with their start and end apart: 16, of which 8 were waited for; matrix products, arithmetic and copies ran while one was open for 1% of the time, Pallas kernels for 24%

profile of v1, /device:TPU:58, one launch (start us, length us, event | category | flops | bytes accessed | tf_op | source)
XLA Modules:
  0.0 306.4 jit_solution(48613334575777943)
XLA Ops:
  0.0 0.8 reduce_sum.9
  0.8 0.8 fusion.4
  1.5 5.4 %collective-permute-start.2 = (f32[3,31]{1,0:T(4,128)S(1)}, f32[3,31]{1,0:T(4,128)S(1)}, u32[]{:S(2)}, u32[]{:S(2)}) collective-permute-start(f32[3,31]{1,0:T(4,128)S(1)} %fusion.4), channel_id=1, source_target_pairs={{0,192},{64,0},{128,64},{192,128},{1,193},{65,1},{129,65},{193,129... | collective-permute-start | bytes 1124 | tf_op jit(solution)/shard_map/ppermute | solution.py:613
  6.9 1.4 collective-permute-start.1
  8.4 2.4 collective-permute-start
  10.8 0.8 fusion.3
  11.5 7.8 %shard_map.55 = bf16[64,400,128]{2,1,0:T(8,128)(2,1)} custom-call(s32[80]{0:T(128)} %bitcast.20, s32[80]{0:T(128)} %bitcast.21, bf16[80,24,1024]{2,1,0:T(8,128)(2,1)} %bitcast.16), custom_call_target="tpu_custom_call" | custom-call | bytes 7864320 | tf_op jit(solution)/shard_map/pallas_call | solution.py:168
  19.3 0.0 collective-permute-done.2
  19.3 0.0 collective-permute-done.1
  19.3 0.0 collective-permute-done
  19.4 9.0 %all-to-all-start = ((bf16[64,400,128]{2,1,0:T(8,128)(2,1)}), bf16[64,400,128]{2,1,0:T(8,128)(2,1)}, u32[]{:S(2)}, u32[]{:S(2)}) async-start(bf16[64,400,128]{2,1,0:T(8,128)(2,1)} %shard_map.55), calls=%async_computation | async-start | bytes 13107200 | tf_op jit(solution)/shard_map/all_to_all | solution.py:625
  28.4 0.6 pad_add_fusion.place
  29.0 0.7 reshape.9.taps
  29.7 3.5 %shard_map.56 = (f32[3,256,384]{2,1,0:T(8,128)}, s16[3,128,384]{2,1,0:T(8,128)(2,1)}, s16[3,128,384]{2,1,0:T(8,128)(2,1)}) custom-call(s32[2]{0:T(128)} %pad_add_fusion.place, f32[24,32,1024]{2,1,0:T(8,128)} %start), custom_call_target="tpu_custom_call" | custom-call | flops 3000000 | bytes 6000000 | tf_op jit(solution)/shard_map/pallas_call | solution.py:371
  33.2 2.0 collective-permute-start.3
  35.3 3.5 %collective-permute-start.4 = (s16[3,128,384]{2,1,0:T(8,128)(2,1)}, s16[3,128,384]{2,1,0:T(8,128)(2,1)S(1)}, u32[]{:S(2)}, u32[]{:S(2)}) collective-permute-start(s16[3,128,384]{2,1,0:T(8,128)(2,1)} %get-tuple-element.42), channel_id=1, source_target_pairs={{1,0},{2,1},{3,2},{4,3},{5,4},{6,5},{7,6},{8,7},{9,8},{10,9},{11,1... | collective-permute-start | bytes 884744 | tf_op jit(solution)/shard_map/ppermute | solution.py:617
  38.8 22.6 %shard_map.58 = (bf16[4,256,512]{2,1,0:T(8,128)(2,1)}, bf16[4,512,256]{2,1,0:T(8,128)(2,1)}, bf16[4,384,384]{2,1,0:T(8,128)(2,1)}, bf16[4,768,384]{2,1,0:T(8,128...) custom-call(f32[4,93]{1,0:T(4,128)} %reshape.9.taps), custom_call_target="tpu_custom_call" | custom-call | flops 4000000000 | bytes 20000000 | tf_op jit(solution)/shard_map/pallas_call | solution.py:335
  61.4 55.7 %all-to-all-done.arrived.whole_arrived = bf16[64,400,128]{2,1,0:T(8,128)(2,1)} async-done(((bf16[64,400,128]{2,1,0:T(8,128)(2,1)}), bf16[64,400,128]{2,1,0:T(8,128)(2,1)}, u32[]{:S(2)}, u32[]{:S(2)}) %all-to-all-start) | async-done | bytes 6553632 | tf_op jit(solution)/shard_map/all_to_all | solution.py:625
  117.0 12.0 %shard_map.57 = (s16[768,384]{1,0:T(8,128)(2,1)}, s16[768,384]{1,0:T(8,128)(2,1)}, s16[768,384]{1,0:T(8,128)(2,1)}, s16[768,384]{1,0:T(8,128)(2,1)}) custom-call(s32[2]{0:T(128)} %pad_add_fusion.place, bf16[64,400,128]{2,1,0:T(8,128)(2,1)} %all-to-all-done.arrived.whole_arrived, bf16[64,400,128]{2,1,0:T(8,128)(2,1)} %all-to-all-done.arrived.whole_arrived), custom_call_target="tpu_custom_call" | custom-call | flops 3276800 | bytes 6553600 | tf_op jit(solution)/shard_map/pallas_call | solution.py:261
  129.0 1.7 collective-permute-start.5
  130.7 4.6 %collective-permute-start.6 = (s16[768,384]{1,0:T(8,128)(2,1)}, s16[768,384]{1,0:T(8,128)(2,1)S(1)}, u32[]{:S(2)}, u32[]{:S(2)}) collective-permute-start(s16[768,384]{1,0:T(8,128)(2,1)} %get-tuple-element.51), channel_id=1, source_target_pairs={{0,128},{64,192},{128,0},{192,64},{1,129},{65,193},{129,1},{193,65... | collective-permute-start | bytes 1769480 | tf_op jit(solution)/shard_map/ppermute | solution.py:613
  135.3 0.0 collective-permute-start.7
  135.3 0.0 collective-permute-done.3.from_left.e_left
  135.3 0.0 copy-start.10
  135.3 0.0 collective-permute-done.4.from_right.e_right
  135.3 0.0 copy-start.11
  135.3 0.7 copy-done.10
  136.0 0.1 copy-done.11
  136.1 8.4 %shard_map.59.blur_ref = f32[4,768,384]{2,1,0:T(8,128)} custom-call(f32[3,256,384]{2,1,0:T(8,128)} %get-tuple-element.40.own, s16[3,128,384]{2,1,0:T(8,128)(2,1)} %copy-done.10, s16[3,128,384]{2,1,0:T(8,128)(2,1)} %copy-done.11, bf16[4,256,512]{2,1,0:T(8,128)(2,1)} %get-tuple-element.45.kx.rest_4_, bf16[4,384,384]{2,1,0:T(8,128)(2,1)} %get-tuple-element.46.ty.rest_6_, ...), custom_call_target="tpu_custom_call" | custom-call | flops 7000000000 | bytes 16000000 | tf_op jit(solution)/shard_map/pallas_call | solution.py:448
  144.5 5.8 %shard_map.60.rest_0_ = f32[3,512,384]{2,1,0:T(8,128)} custom-call(s32[2]{0:T(128)} %pad_add_fusion.place, s16[768,384]{1,0:T(8,128)(2,1)} %get-tuple-element.53.code.rest_0_, f32[4,768,384]{2,1,0:T(8,128)} %shard_map.59.blur_ref, bf16[4,512,256]{2,1,0:T(8,128)(2,1)} %get-tuple-element.48.kxt.rest_5_, bf16[4,768,384]{2,1,0:T(8,128)(2,1)} %get-tuple-element.49.tyt.rest_7_, ...), custom_call_target="tpu_custom_call" | custom-call | flops 2000000000 | bytes 8000000 | tf_op jit(solution)/shard_map/pallas_call | solution.py:487
  150.3 31.0 %collective-permute-done.7.code.rest_1_ = s16[768,384]{1,0:T(8,128)(2,1)S(1)} collective-permute-done((s16[768,384]{1,0:T(8,128)(2,1)}, s16[768,384]{1,0:T(8,128)(2,1)S(1)}, u32[]{:S(2)}, u32[]{:S(2)}) %collective-permute-start.7) | collective-permute-done | bytes 589856 | tf_op jit(solution)/shard_map/ppermute | solution.py:613
  181.3 0.0 copy-start.2
  181.3 0.8 copy-done.2
  182.1 6.6 %shard_map.61.rest_0_ = f32[3,512,384]{2,1,0:T(8,128)} custom-call(s32[2]{0:T(128)} %pad_add_fusion.place, s16[768,384]{1,0:T(8,128)(2,1)} %copy-done.2, f32[4,768,384]{2,1,0:T(8,128)} %shard_map.59.blur_ref, bf16[4,512,256]{2,1,0:T(8,128)(2,1)} %get-tuple-element.48.kxt.rest_5_, bf16[4,768,384]{2,1,0:T(8,128)(2,1)} %get-tuple-element.49.tyt.rest_7_, ...), custom_call_target="tpu_custom_call" | custom-call | flops 2000000000 | bytes 8000000 | tf_op jit(solution)/shard_map/pallas_call | solution.py:487
  188.8 0.0 collective-permute-done.6.code.rest_2_
  188.8 0.8 copy-done.1
  189.6 6.7 %shard_map.62.rest_0_ = f32[3,512,384]{2,1,0:T(8,128)} custom-call(s32[2]{0:T(128)} %pad_add_fusion.place, s16[768,384]{1,0:T(8,128)(2,1)} %copy-done.1, f32[4,768,384]{2,1,0:T(8,128)} %shard_map.59.blur_ref, bf16[4,512,256]{2,1,0:T(8,128)(2,1)} %get-tuple-element.48.kxt.rest_5_, bf16[4,768,384]{2,1,0:T(8,128)(2,1)} %get-tuple-element.49.tyt.rest_7_, ...), custom_call_target="tpu_custom_call" | custom-call | flops 2000000000 | bytes 8000000 | tf_op jit(solution)/shard_map/pallas_call | solution.py:487
  196.3 0.0 collective-permute-done.5.code.rest_3_
  196.3 0.9 copy-done
  197.1 7.5 %shard_map.63 = (f32[3,512,384]{2,1,0:T(8,128)}, s16[784,384]{1,0:T(8,128)(2,1)}, s16[784,384]{1,0:T(8,128)(2,1)}) custom-call(s32[2]{0:T(128)} %pad_add_fusion.place, s16[768,384]{1,0:T(8,128)(2,1)} %copy-done, f32[4,768,384]{2,1,0:T(8,128)} %shard_map.59.blur_ref, bf16[4,512,256]{2,1,0:T(8,128)(2,1)} %get-tuple-element.48.kxt.rest_5_, ...), custom_call_target="tpu_custom_call" | custom-call | flops 2000000000 | bytes 8000000 | tf_op jit(solution)/shard_map/pallas_call | solution.py:487
  204.6 1.9 collective-permute-start.8
  206.5 3.6 %collective-permute-start.9 = (s16[784,384]{1,0:T(8,128)(2,1)}, s16[784,384]{1,0:T(8,128)(2,1)S(1)}, u32[]{:S(2)}, u32[]{:S(2)}) collective-permute-start(s16[784,384]{1,0:T(8,128)(2,1)} %get-tuple-element.56), channel_id=1, source_target_pairs={{1,0},{2,1},{3,2},{4,3},{5,4},{6,5},{7,6},{8,7},{9,8},{10,9},{11,1... | collective-permute-start | bytes 1806344 | tf_op jit(solution)/shard_map/ppermute | solution.py:617
  210.2 12.4 %collective-permute-done.8.x_left = s16[784,384]{1,0:T(8,128)(2,1)S(1)} collective-permute-done((s16[784,384]{1,0:T(8,128)(2,1)}, s16[784,384]{1,0:T(8,128)(2,1)S(1)}, u32[]{:S(2)}, u32[]{:S(2)}) %collective-permute-start.8) | collective-permute-done | bytes 602144 | tf_op jit(solution)/shard_map/ppermute | solution.py:617
  222.5 0.0 collective-permute-done.9.x_right
  222.5 0.8 copy-done.8
  223.3 0.2 copy-done.9
  223.6 22.3 %shard_map.64 = (f32[3,256,256]{2,1,0:T(8,128)}, f32[3,256,256]{2,1,0:T(8,128)}, s16[400,256]{1,0:T(8,128)(2,1)}, s16[400,256]{1,0:T(8,128)(2,1)}) custom-call(s32[2]{0:T(128)} %pad_add_fusion.place, f32[3,256,384]{2,1,0:T(8,128)} %get-tuple-element.40.own, s16[3,128,384]{2,1,0:T(8,128)(2,1)} %copy-done.10, s16[3,128,384]{2,1,0:T(8,128)(2,1)} %copy-done.11, ...), custom_call_target="tpu_custom_call" | custom-call | flops 16000000000 | bytes 40000000 | tf_op jit(solution)/shard_map/pallas_call | solution.py:545
  245.9 1.9 collective-permute-start.10
  247.8 3.6 %collective-permute-start.11 = (s16[400,256]{1,0:T(8,128)(2,1)}, s16[400,256]{1,0:T(8,128)(2,1)S(1)}, u32[]{:S(2)}, u32[]{:S(2)}) collective-permute-start(s16[400,256]{1,0:T(8,128)(2,1)} %get-tuple-element.60), channel_id=1, source_target_pairs={{1,0},{2,1},{3,2},{4,3},{5,4},{6,5},{7,6},{8,7},{9,8},{10,9},{11,1... | collective-permute-start | bytes 614408 | tf_op jit(solution)/shard_map/ppermute | solution.py:617
  251.4 1.7 collective-permute-done.10.x_left
  253.1 1.9 collective-permute-done.11.x_right
  255.0 0.0 copy-done.6
  255.0 0.7 copy-done.7
  255.7 2.7 shard_map.65.rest_0_
  258.4 1.4 collective-permute-start.14
  259.7 4.5 %collective-permute-start.13 = (s16[784,256]{1,0:T(8,128)(2,1)}, s16[784,256]{1,0:T(8,128)(2,1)S(1)}, u32[]{:S(2)}, u32[]{:S(2)}) collective-permute-start(s16[784,256]{1,0:T(8,128)(2,1)} %shard_map.65.rest_0_), channel_id=1, source_target_pairs={{0,128},{64,192},{128,0},{192,64},{1,129},{65,193},{129,1},{193,65... | collective-permute-start | bytes 1204232 | tf_op jit(solution)/shard_map/ppermute | solution.py:613
  264.2 0.0 collective-permute-start.12
  264.2 10.0 %collective-permute-done.14.rest_3_ = s16[784,256]{1,0:T(8,128)(2,1)S(1)} collective-permute-done((s16[784,256]{1,0:T(8,128)(2,1)}, s16[784,256]{1,0:T(8,128)(2,1)S(1)}, u32[]{:S(2)}, u32[]{:S(2)}) %collective-permute-start.14) | collective-permute-done | bytes 401440 | tf_op jit(solution)/shard_map/ppermute | solution.py:613
  274.2 23.8 %collective-permute-done.13.rest_2_ = s16[784,256]{1,0:T(8,128)(2,1)S(1)} collective-permute-done((s16[784,256]{1,0:T(8,128)(2,1)}, s16[784,256]{1,0:T(8,128)(2,1)S(1)}, u32[]{:S(2)}, u32[]{:S(2)}) %collective-permute-start.13) | collective-permute-done | bytes 401440 | tf_op jit(solution)/shard_map/ppermute | solution.py:613
  298.0 3.5 %collective-permute-done.12.rest_1_ = s16[784,256]{1,0:T(8,128)(2,1)S(1)} collective-permute-done((s16[784,256]{1,0:T(8,128)(2,1)}, s16[784,256]{1,0:T(8,128)(2,1)S(1)}, u32[]{:S(2)}, u32[]{:S(2)}) %collective-permute-start.12) | collective-permute-done | bytes 401440 | tf_op jit(solution)/shard_map/ppermute | solution.py:613
  301.5 0.0 copy-done.3
  301.5 0.0 copy-done.4
  301.6 0.8 copy-done.5
  302.3 4.1 %shard_map.66 = f32[24,32,1024]{2,1,0:T(8,128)} custom-call(s32[2]{0:T(128)} %pad_add_fusion.place, s16[784,256]{1,0:T(8,128)(2,1)} %shard_map.65.rest_0_, s16[784,256]{1,0:T(8,128)(2,1)} %copy-done.5, s16[784,256]{1,0:T(8,128)(2,1)} %copy-done.4, s16[784,256]{1,0:T(8,128)(2,1)} %copy-done.3), custom_call_target="tpu_custom_call" | custom-call | flops 3000000 | bytes 6000000 | tf_op jit(solution)/shard_map/pallas_call | solution.py:595
  (10 shorter events, 0.0 us)
Async XLA Ops:
  1.5 17.8 %collective-permute-start.2 = (f32[3,31]{1,0:T(4,128)S(1)}, f32[3,31]{1,0:T(4,128)S(1)}, u32[]{:S(2)}, u32[]{:S(2)}) collective-permute-start(f32[3,31]{1,0:T(4,128)S(1)} %fusion.4), channel_id=1, source_target_pairs={{0,192},{64,0},{128,64},{192,128},{1,193},{65,1},{129,65},{193,129... | collective-permute-start | bytes 1124 | tf_op jit(solution)/shard_map/ppermute | solution.py:613
  6.9 12.4 %collective-permute-start.1 = (f32[3,31]{1,0:T(4,128)S(1)}, f32[3,31]{1,0:T(4,128)S(1)}, u32[]{:S(2)}, u32[]{:S(2)}) collective-permute-start(f32[3,31]{1,0:T(4,128)S(1)} %fusion.4), channel_id=1, source_target_pairs={{0,128},{64,192},{128,0},{192,64},{1,129},{65,193},{129,1},{193,65... | collective-permute-start | bytes 1124 | tf_op jit(solution)/shard_map/ppermute | solution.py:613
  8.4 11.0 %collective-permute-start = (f32[3,31]{1,0:T(4,128)S(1)}, f32[3,31]{1,0:T(4,128)S(1)}, u32[]{:S(2)}, u32[]{:S(2)}) collective-permute-start(f32[3,31]{1,0:T(4,128)S(1)} %fusion.4), channel_id=1, source_target_pairs={{0,64},{64,128},{128,192},{192,0},{1,65},{65,129},{129,193},{193,1... | collective-permute-start | bytes 1124 | tf_op jit(solution)/shard_map/ppermute | solution.py:613
  19.4 97.7 %all-to-all-start = ((bf16[64,400,128]{2,1,0:T(8,128)(2,1)}), bf16[64,400,128]{2,1,0:T(8,128)(2,1)}, u32[]{:S(2)}, u32[]{:S(2)}) async-start(bf16[64,400,128]{2,1,0:T(8,128)(2,1)} %shard_map.55), calls=%async_computation | async-start | bytes 13107200 | tf_op jit(solution)/shard_map/all_to_all | solution.py:625
  33.2 102.1 %collective-permute-start.3 = (s16[3,128,384]{2,1,0:T(8,128)(2,1)}, s16[3,128,384]{2,1,0:T(8,128)(2,1)S(1)}, u32[]{:S(2)}, u32[]{:S(2)}) collective-permute-start(s16[3,128,384]{2,1,0:T(8,128)(2,1)} %get-tuple-element.41), channel_id=1, source_target_pairs={{0,1},{1,2},{2,3},{3,4},{4,5},{5,6},{6,7},{7,8},{8,9},{9,10},{10,1... | collective-permute-start | bytes 884744 | tf_op jit(solution)/shard_map/ppermute | solution.py:617
  35.3 100.1 %collective-permute-start.4 = (s16[3,128,384]{2,1,0:T(8,128)(2,1)}, s16[3,128,384]{2,1,0:T(8,128)(2,1)S(1)}, u32[]{:S(2)}, u32[]{:S(2)}) collective-permute-start(s16[3,128,384]{2,1,0:T(8,128)(2,1)} %get-tuple-element.42), channel_id=1, source_target_pairs={{1,0},{2,1},{3,2},{4,3},{5,4},{6,5},{7,6},{8,7},{9,8},{10,9},{11,1... | collective-permute-start | bytes 884744 | tf_op jit(solution)/shard_map/ppermute | solution.py:617
  129.0 67.2 %collective-permute-start.5 = (s16[768,384]{1,0:T(8,128)(2,1)}, s16[768,384]{1,0:T(8,128)(2,1)S(1)}, u32[]{:S(2)}, u32[]{:S(2)}) collective-permute-start(s16[768,384]{1,0:T(8,128)(2,1)} %get-tuple-element.43), channel_id=1, source_target_pairs={{0,192},{64,0},{128,64},{192,128},{1,193},{65,1},{129,65},{193,129... | collective-permute-start | bytes 1769480 | tf_op jit(solution)/shard_map/ppermute | solution.py:613
  130.7 58.1 %collective-permute-start.6 = (s16[768,384]{1,0:T(8,128)(2,1)}, s16[768,384]{1,0:T(8,128)(2,1)S(1)}, u32[]{:S(2)}, u32[]{:S(2)}) collective-permute-start(s16[768,384]{1,0:T(8,128)(2,1)} %get-tuple-element.51), channel_id=1, source_target_pairs={{0,128},{64,192},{128,0},{192,64},{1,129},{65,193},{129,1},{193,65... | collective-permute-start | bytes 1769480 | tf_op jit(solution)/shard_map/ppermute | solution.py:613
  135.3 46.0 %collective-permute-start.7 = (s16[768,384]{1,0:T(8,128)(2,1)}, s16[768,384]{1,0:T(8,128)(2,1)S(1)}, u32[]{:S(2)}, u32[]{:S(2)}) collective-permute-start(s16[768,384]{1,0:T(8,128)(2,1)} %get-tuple-element.52), channel_id=1, source_target_pairs={{0,64},{64,128},{128,192},{192,0},{1,65},{65,129},{129,193},{193,1... | collective-permute-start | bytes 1769480 | tf_op jit(solution)/shard_map/ppermute | solution.py:613
  135.3 0.7 copy-start.10
  135.3 0.8 copy-start.11
  181.3 0.8 copy-start.2
  188.8 0.8 copy-start.1
  196.3 0.9 copy-start
  204.6 17.9 %collective-permute-start.8 = (s16[784,384]{1,0:T(8,128)(2,1)}, s16[784,384]{1,0:T(8,128)(2,1)S(1)}, u32[]{:S(2)}, u32[]{:S(2)}) collective-permute-start(s16[784,384]{1,0:T(8,128)(2,1)} %get-tuple-element.55), channel_id=1, source_target_pairs={{0,1},{1,2},{2,3},{3,4},{4,5},{5,6},{6,7},{7,8},{8,9},{9,10},{10,1... | collective-permute-start | bytes 1806344 | tf_op jit(solution)/shard_map/ppermute | solution.py:617
  206.5 16.0 %collective-permute-start.9 = (s16[784,384]{1,0:T(8,128)(2,1)}, s16[784,384]{1,0:T(8,128)(2,1)S(1)}, u32[]{:S(2)}, u32[]{:S(2)}) collective-permute-start(s16[784,384]{1,0:T(8,128)(2,1)} %get-tuple-element.56), channel_id=1, source_target_pairs={{1,0},{2,1},{3,2},{4,3},{5,4},{6,5},{7,6},{8,7},{9,8},{10,9},{11,1... | collective-permute-start | bytes 1806344 | tf_op jit(solution)/shard_map/ppermute | solution.py:617
  222.5 0.8 copy-start.8
  222.5 1.0 copy-start.9
  245.9 7.3 %collective-permute-start.10 = (s16[400,256]{1,0:T(8,128)(2,1)}, s16[400,256]{1,0:T(8,128)(2,1)S(1)}, u32[]{:S(2)}, u32[]{:S(2)}) collective-permute-start(s16[400,256]{1,0:T(8,128)(2,1)} %get-tuple-element.59), channel_id=1, source_target_pairs={{0,1},{1,2},{2,3},{3,4},{4,5},{5,6},{6,7},{7,8},{8,9},{9,10},{10,1... | collective-permute-start | bytes 614408 | tf_op jit(solution)/shard_map/ppermute | solution.py:617
  247.8 7.2 %collective-permute-start.11 = (s16[400,256]{1,0:T(8,128)(2,1)}, s16[400,256]{1,0:T(8,128)(2,1)S(1)}, u32[]{:S(2)}, u32[]{:S(2)}) collective-permute-start(s16[400,256]{1,0:T(8,128)(2,1)} %get-tuple-element.60), channel_id=1, source_target_pairs={{1,0},{2,1},{3,2},{4,3},{5,4},{6,5},{7,6},{8,7},{9,8},{10,9},{11,1... | collective-permute-start | bytes 614408 | tf_op jit(solution)/shard_map/ppermute | solution.py:617
  253.1 1.9 copy-start.6
  255.0 0.7 copy-start.7
  258.4 15.9 %collective-permute-start.14 = (s16[784,256]{1,0:T(8,128)(2,1)}, s16[784,256]{1,0:T(8,128)(2,1)S(1)}, u32[]{:S(2)}, u32[]{:S(2)}) collective-permute-start(s16[784,256]{1,0:T(8,128)(2,1)} %shard_map.65.rest_0_), channel_id=1, source_target_pairs={{0,192},{64,0},{128,64},{192,128},{1,193},{65,1},{129,65},{193,129... | collective-permute-start | bytes 1204232 | tf_op jit(solution)/shard_map/ppermute | solution.py:613
  259.7 38.3 %collective-permute-start.13 = (s16[784,256]{1,0:T(8,128)(2,1)}, s16[784,256]{1,0:T(8,128)(2,1)S(1)}, u32[]{:S(2)}, u32[]{:S(2)}) collective-permute-start(s16[784,256]{1,0:T(8,128)(2,1)} %shard_map.65.rest_0_), channel_id=1, source_target_pairs={{0,128},{64,192},{128,0},{192,64},{1,129},{65,193},{129,1},{193,65... | collective-permute-start | bytes 1204232 | tf_op jit(solution)/shard_map/ppermute | solution.py:613
  264.2 37.3 %collective-permute-start.12 = (s16[784,256]{1,0:T(8,128)(2,1)}, s16[784,256]{1,0:T(8,128)(2,1)S(1)}, u32[]{:S(2)}, u32[]{:S(2)}) collective-permute-start(s16[784,256]{1,0:T(8,128)(2,1)} %shard_map.65.rest_0_), channel_id=1, source_target_pairs={{0,64},{64,128},{128,192},{192,0},{1,65},{65,129},{129,193},{193,1... | collective-permute-start | bytes 1204232 | tf_op jit(solution)/shard_map/ppermute | solution.py:613
  274.2 27.3 %copy-start.3 = (s16[784,256]{1,0:T(8,128)(2,1)}, s16[784,256]{1,0:T(8,128)(2,1)S(1)}, u32[]{:S(2)}) copy-start(s16[784,256]{1,0:T(8,128)(2,1)S(1)} %collective-permute-done.14.rest_3_) | copy-start | bytes 1204228
  298.0 3.5 %copy-start.4 = (s16[784,256]{1,0:T(8,128)(2,1)}, s16[784,256]{1,0:T(8,128)(2,1)S(1)}, u32[]{:S(2)}) copy-start(s16[784,256]{1,0:T(8,128)(2,1)S(1)} %collective-permute-done.13.rest_2_) | copy-start | bytes 1204228
  301.6 0.8 copy-start.5

commit v2 on v1

v2 whole, which is shorter than its diff:
```python
import functools

import jax
import jax.numpy as jnp
import numpy as np
from jax import lax
from jax.experimental import pallas as pl
from jax.experimental.pallas import tpu as pltpu
from jax.sharding import PartitionSpec as P

ITERS = 2
TAPS = 31
HALF = 15
VIEWS = 4
NZ = 24
BX = 32
MARGIN = 16
EX = BX + 2 * MARGIN
YQ = 256
YE = 384
TURN = 320
ROWS = BX * NZ
ZI = 8
ZG = NZ // ZI
XR = BX * ZI
EXR = EX * ZI
GX = 8
GR = GX * ZI
ZR = GX * NZ
FULL = 32700.0
STEPS = 128.0
LN2 = float(np.log(2.0))
M_MID, M_SCALE = 2.125, 32767.0 / 1.875
E_SCALE = 32767.0 / 2.0
VMEM = 28 * 1024 * 1024

f32, bf16, i32, i16 = jnp.float32, jnp.bfloat16, jnp.int32, jnp.int16


def params(limit=VMEM):
    return pltpu.CompilerParams(vmem_limit_bytes=limit)


KEPT = pl.BlockSpec(memory_space=pltpu.VMEM)


def kept(operands):
    return [pltpu.with_memory_space_constraint(x, pltpu.VMEM) for x in operands]


def cost(flops, moved):
    return pl.CostEstimate(flops=int(flops), bytes_accessed=int(moved), transcendentals=0)


def dot(a, b):
    return jnp.dot(a, b, preferred_element_type=f32)


def to_code(x):
    return jnp.floor(x + 0.5).astype(i32).astype(i16)


def from_code(c):
    return c.astype(i32).astype(f32)


def scale_steps(top):
    return jnp.ceil(jnp.log(jnp.maximum(top, 1e-30)) * (STEPS / LN2))


def lane_code(value):
    k = scale_steps(jnp.max(jnp.abs(value), axis=0, keepdims=True))
    code = to_code(value * (jnp.exp(k * (-LN2 / STEPS)) * FULL))
    return code, jnp.broadcast_to(k, (16, value.shape[1])).astype(i32).astype(i16)


def lane_value(ref):
    n = ref.shape[0] - 16
    k = from_code(ref[n:])[0:1]
    return from_code(ref[:n]) * (jnp.exp(k * (LN2 / STEPS)) * (1.0 / FULL))


def send(ref, value):
    n = value.shape[0]
    ref[:n], ref[n:] = lane_code(value)


def flat(x):
    return x.reshape(x.shape[0] * x.shape[1], x.shape[2])


LOADS = 4
SLOT = NZ * 8


def pack_body(cap, blocks, columns, tiles, out, labels, count, slots, held, sent, loaded, pushed):
    pieces = tiles.shape[0]
    part = pieces // LOADS
    groups = out.shape[0]

    def load(i):
        rows = pl.ds(i * part, part)
        return pltpu.make_async_copy(tiles.at[rows], held.at[rows], loaded.at[i])

    for i in range(LOADS):
        load(i).start()

    def clear(i, _):
        labels[i] = 0
        return 0

    lax.fori_loop(0, groups * cap, clear, 0)

    def zero(i, _):
        count[i] = 0
        return 0

    lax.fori_loop(0, groups, zero, 0)

    def route(p, _):
        b = blocks[p]
        rank = count[b]
        count[b] = rank + 1
        slot = b * cap + rank
        labels[slot] = columns[p] + 1
        slots[p] = slot
        return 0

    lax.fori_loop(0, pieces, route, 0)
    lane = lax.broadcasted_iota(i32, (16, 128), 1)

    def mark(b, _):
        row = jnp.zeros((16, 128), i32)
        for rank in range(cap):
            row = jnp.where(lane == rank, labels[b * cap + rank], row)
        sent[b, cap * SLOT :, :] = row.astype(f32).astype(bf16)
        return 0

    lax.fori_loop(0, groups, mark, 0)
    def push(b, at, rows, sem):
        part = pl.ds(pl.multiple_of(at, 16), rows)
        return pltpu.make_async_copy(sent.at[b, part, :], out.at[b, part, :], sem)

    def tags():
        rows = pl.ds(cap * SLOT, 16)
        return pltpu.make_async_copy(sent.at[:, rows, :], out.at[:, rows, :], pushed.at[1])

    tags().start()
    for i in range(LOADS):
        load(i).wait()

        def put(p, _):
            slot = slots[p]
            b = slot // cap
            at = (slot - b * cap) * SLOT
            for c in range(8):
                rows = pl.ds(pl.multiple_of(at + 16 * c, 16), 16)
                sent[b, rows, :] = held[p, :16, 128 * c : 128 * (c + 1)]
            for c in range(0, 8, 2):
                rows = pl.ds(pl.multiple_of(at + 128 + 8 * c, 16), 16)
                sent[b, rows, :] = jnp.concatenate(
                    [
                        held[p, 16:, 128 * c : 128 * (c + 1)],
                        held[p, 16:, 128 * (c + 1) : 128 * (c + 2)],
                    ],
                    axis=0,
                )
            push(b, at, SLOT, pushed.at[0]).start()
            return 0

        lax.fori_loop(i * part, (i + 1) * part, put, 0, unroll=2)
    tags().wait()
    if pieces % cap == 0:
        every = pl.ds(0, pieces // cap), pl.ds(0, cap * SLOT)
        pltpu.make_async_copy(sent.at[every], out.at[every], pushed.at[0]).wait()
    else:
        lax.fori_loop(0, pieces, lambda p, _: push(0, 0, SLOT, pushed.at[0]).wait(), None)


def pack(cap, groups, blocks, columns, tiles):
    smem = pl.BlockSpec(memory_space=pltpu.SMEM)
    message = (groups, cap * SLOT + 16, 128)
    return pl.pallas_call(
        functools.partial(pack_body, cap),
        out_shape=pltpu.HBM(message, bf16),
        in_specs=[smem, smem, pl.BlockSpec(memory_space=pltpu.HBM)],
        out_specs=pl.BlockSpec(memory_space=pltpu.HBM),
        scratch_shapes=[
            pltpu.SMEM((groups * cap,), i32),
            pltpu.SMEM((groups,), i32),
            pltpu.SMEM((tiles.shape[0],), i32),
            pltpu.VMEM(tiles.shape, bf16),
            pltpu.VMEM(message, bf16),
            pltpu.SemaphoreType.DMA((LOADS,)),
            pltpu.SemaphoreType.DMA((2,)),
        ],
        compiler_params=params(2 * VMEM),
        cost_estimate=cost(0, 4 * tiles.size),
    )(blocks, columns, pltpu.with_memory_space_constraint(tiles, pltpu.HBM))


PART_VIEWS = (0, 1, 2, 2, 3)
PART_ROWS = (0, 0, 0, ROWS // 2, 0)


def unpack_body(cap, chunk, place, arrived, whole_arrived, *rest):
    outs, (acc, codes, count, marks, table, labels, sem) = rest[: VIEWS + 1], rest[VIEWS + 1 :]
    step = pl.program_id(0)
    layer = place[1]

    @pl.when(step == 0)
    def _():
        fetch = pltpu.make_async_copy(
            whole_arrived.at[:, pl.ds(cap * SLOT, 16), :], marks, sem.at[0]
        )
        fetch.start()
        acc[...] = jnp.zeros_like(acc)

        def zero(i, _):
            count[i] = 0
            return 0

        lax.fori_loop(0, BX, zero, 0)
        fetch.wait()
        ranks = table.shape[0]
        which = jnp.where(iota((ranks, 128), 0) == iota((ranks, 128), 1), 1.0, 0.0)
        lines = jnp.max(marks[...].astype(f32), axis=1)
        found = lax.dot_general(which, lines, (((1,), (1,)), ((), ())), preferred_element_type=f32)
        table[:, : lines.shape[0]] = found.astype(i32)
        move = pltpu.make_async_copy(table, labels, sem.at[1])
        move.start()
        move.wait()

    for j in range(chunk):
        for rank in range(cap):
            label = labels[rank, step * chunk + j]

            @pl.when(label > 0)
            def _():
                col = label - 1
                rows = pl.ds(pl.multiple_of(col * ZI, ZI), ZI)
                tile = arrived[j, rank * SLOT : (rank + 1) * SLOT, :].astype(f32)
                for c in range(8):
                    lanes = slice(128 * c, 128 * (c + 1))
                    acc[0, rows, lanes] += tile[16 * c : 16 * c + 8]
                    acc[1, rows, lanes] += tile[16 * c + 8 : 16 * c + 16]
                    acc[2, rows, lanes] += tile[128 + 8 * c : 136 + 8 * c]
                count[col] += 1

    @pl.when(step == pl.num_programs(0) - 1)
    def _():
        row = lax.broadcasted_iota(i32, (2 * ZI, 128), 0)
        lane = lax.broadcasted_iota(i32, (2 * ZI, 128), 1)

        def pair(i, _):
            first = M_SCALE / jnp.maximum(count[2 * i], 1).astype(f32)
            second = M_SCALE / jnp.maximum(count[2 * i + 1], 1).astype(f32)
            inverse = jnp.where(row < ZI, first, second)
            for g in range(ZG):
                rows = pl.ds(pl.multiple_of(i * 2 * ZI, 2 * ZI), 2 * ZI)
                to = pl.ds(pl.multiple_of(g * XR + i * 2 * ZI, 2 * ZI), 2 * ZI)
                blocks = [
                    acc[g, rows, 128 * c : 128 * (c + 1)] * inverse - M_MID * M_SCALE
                    for c in range(2 * VIEWS)
                ]
                for v in range(VIEWS):
                    after = blocks[min(2 * v + 2, 2 * VIEWS - 1)]
                    before = blocks[max(2 * v - 1, 0)]
                    ends = jnp.where(lane < 64, after, before)
                    code = jnp.concatenate([blocks[2 * v], blocks[2 * v + 1], ends], axis=1)
                    codes[v, to, :] = to_code(code)
            return 0

        lax.fori_loop(0, BX // 2, pair, 0, unroll=4)
        for r, at, out in zip(PART_VIEWS, PART_ROWS, outs):
            out[...] = codes[lax.rem(layer + r, VIEWS), at : at + out.shape[0], :]


def unpack(cap, place, arrived):
    groups = arrived.shape[0]
    chunk = min(32, groups)
    shapes = [(ROWS // PART_VIEWS.count(r), YE) for r in PART_VIEWS]
    smem = pl.BlockSpec(memory_space=pltpu.SMEM)
    return pl.pallas_call(
        functools.partial(unpack_body, cap, chunk),
        grid=(groups // chunk,),
        out_shape=tuple(jax.ShapeDtypeStruct(shape, i16) for shape in shapes),
        in_specs=[
            smem,
            pl.BlockSpec((chunk,) + arrived.shape[1:], lambda s: (s, 0, 0)),
            pl.BlockSpec(memory_space=pl.ANY),
        ],
        out_specs=tuple(pl.BlockSpec(shape, lambda s: (0, 0)) for shape in shapes),
        scratch_shapes=[
            pltpu.VMEM((ZG, XR, VIEWS * YQ), f32),
            pltpu.VMEM((VIEWS, ROWS, YE), i16),
            pltpu.SMEM((BX,), i32),
            pltpu.VMEM((groups, 16, 128), bf16),
            pltpu.VMEM((max(8, cap), 128), i32),
            pltpu.SMEM((max(8, cap), 128), i32),
            pltpu.SemaphoreType.DMA((2,)),
        ],
        compiler_params=params(),
        cost_estimate=cost(arrived.size, 2 * arrived.size),
    )(place, arrived, arrived)


def iota(shape, dim):
    return lax.broadcasted_iota(i32, shape, dim)


def bands_body(taps, kx, kxt, ty, tyt, bz, bzt):
    r = pl.program_id(0)

    def band(distance, axis):
        out = jnp.zeros(distance.shape, f32)
        for t in range(TAPS):
            out = jnp.where(distance == t, taps[r, axis * TAPS + t], out)
        return out

    def circulant(row, n):
        wide = jnp.broadcast_to(row[0:1], (n, row.shape[1]))
        return pltpu.roll(wide, 0, 1, stride=1, stride_axis=0).astype(bf16)

    m = iota((8, EXR), 1)
    aligned = lax.bitwise_and(m, ZI - 1) == 0
    taps_at = band(lax.shift_right_logical(m, 3) - 1, 1)
    kx[r] = circulant(jnp.where(aligned, taps_at, 0.0), XR)
    taps_at = band(lax.shift_right_logical(EXR - m, 3) - 1, 1)
    kxt[r] = circulant(jnp.where(aligned, taps_at, 0.0), EXR)[:, :XR]
    n = iota((8, YE), 1)
    apart = jnp.where(n < YE // 2, n, n - YE)
    ty[r] = circulant(band(HALF - apart, 2), YE)
    back = circulant(band(HALF + apart, 2), YE)
    tyt[r] = back

    def parts(x):
        group = jnp.where(x >= 2 * GR, 2, jnp.where(x >= GR, 1, 0))
        within = x - group * GR
        return group * ZI + lax.bitwise_and(within, ZI - 1), lax.shift_right_logical(within, 3)

    (zr, xr), (zc, xc) = parts(iota((ZR, 1), 0)), parts(iota((1, ZR), 1))
    same = xr == xc
    bz[r] = jnp.where(same, band(zc - zr + HALF, 0), 0.0).astype(bf16)
    bzt[r] = jnp.where(same, band(zr - zc + HALF, 0), 0.0).astype(bf16)


MATS = [(XR, EXR), (EXR, XR), (YE, YE), (YE, YE), (ZR, ZR), (ZR, ZR)]


def bands(taps):
    return pl.pallas_call(
        bands_body,
        grid=(VIEWS,),
        out_shape=tuple(pltpu.VMEM((VIEWS,) + s, bf16) for s in MATS),
        in_specs=[pl.BlockSpec(memory_space=pltpu.SMEM)],
        out_specs=(KEPT,) * len(MATS),
        compiler_params=params(),
        cost_estimate=cost(4e9, 2e7),
    )(taps)


def cell_body(place, start, own, left, right, scratch):
    layer = place[1]
    last = start.shape[2] - 128
    after = jnp.minimum((layer + 1) * YQ, last)
    before = jnp.maximum(layer * YQ - 128, 0)
    lane = iota((BX, 128), 1)
    for z in range(NZ):
        rows = pl.ds(z // ZI * XR + z % ZI, BX, stride=ZI)
        for c in range(2):
            at = pl.multiple_of(layer * YQ + c * 128, 128)
            scratch[c, rows, :] = start[z, :, pl.ds(at, 128)]
        head = start[z, :, pl.ds(pl.multiple_of(after, 128), 128)]
        tail = start[z, :, pl.ds(pl.multiple_of(before, 128), 128)]
        head = jnp.where((lane < TURN - YQ) & (layer < VIEWS - 1), head, 0.0)
        tail = jnp.where((lane >= TURN - YQ) & (layer > 0), tail, 0.0)
        scratch[2, rows, :] = head + tail
    value = jnp.concatenate([scratch[c] for c in range(3)], axis=1)
    own[...] = value.reshape(ZG, XR, YE)
    code = to_code(value * E_SCALE).reshape(ZG, XR, YE)
    left[...] = code[:, : XR // 2]
    right[...] = code[:, XR // 2 :]


def cell(place, start):
    half = jax.ShapeDtypeStruct((ZG, XR // 2, YE), i16)
    return pl.pallas_call(
        cell_body,
        out_shape=(pltpu.VMEM((ZG, XR, YE), f32), half, half),
        in_specs=[
            pl.BlockSpec(memory_space=pltpu.SMEM),
            pl.BlockSpec(memory_space=pltpu.VMEM),
        ],
        scratch_shapes=[pltpu.VMEM((3, ROWS, 128), f32)],
        compiler_params=params(),
        cost_estimate=cost(3e6, 6e6),
    )(place, start)


def blurred_columns(field, kx, out):
    for g in range(ZG):
        x = dot(kx[...].reshape(VIEWS * XR, EXR), field[g]).astype(bf16)
        out[:, g * XR : (g + 1) * XR, :] = x.reshape(VIEWS, XR, YE)


def blurred(x, ty, bz):
    y = dot(x, ty).astype(bf16)
    return [dot(bz, columns_of(y, XR, c)) for c in range(BX // GX)]


def columns_of(rows, stride, c):
    return jnp.concatenate(
        [rows[g * stride + c * GR : g * stride + (c + 1) * GR] for g in range(ZG)], axis=0
    )


def rows_from(groups):
    return jnp.concatenate(
        [part[g * GR : (g + 1) * GR] for g in range(ZG) for part in groups], axis=0
    )


def mirrored(quotient, kxt, tyt, bzt, out, first):
    y = dot(quotient, tyt).astype(bf16)
    x = [dot(kxt, y[g * XR : (g + 1) * XR]).astype(bf16) for g in range(ZG)]
    for c in range(EX // GX):
        rows = slice(c * GR, (c + 1) * GR)
        z = dot(bzt, jnp.concatenate([part[rows] for part in x], axis=0))
        for g in range(ZG):
            part = z[g * GR : (g + 1) * GR]
            out[g, rows, :] = part if first else out[g, rows, :] + part


def quotient_of(layer, code, blur_now):
    lane = iota(code.shape, 1)
    inside = (lane < YQ) | ((lane < TURN) & (layer < VIEWS - 1)) | ((lane >= TURN) & (layer > 0))
    measured = jnp.where(inside, from_code(code) * (1.0 / M_SCALE) + M_MID, 0.0)
    return (measured / jnp.where(inside, blur_now, 1.0)).astype(bf16)


def widened(own, from_left, from_right):
    inverse = 1.0 / E_SCALE
    return jnp.concatenate(
        [from_code(from_left) * inverse, own, from_code(from_right) * inverse], axis=1
    )


def blur_body(own, from_left, from_right, kx, ty, bz, out, field, columns):
    step = pl.program_id(0)

    @pl.when(step == 0)
    def _():
        field[...] = widened(own[...], from_left[...], from_right[...]).astype(bf16)
        blurred_columns(field, kx, columns)

    out[step] = rows_from(blurred(columns[step], ty[step], bz[step]))


def blur(own, from_left, from_right, mats):
    operands = kept([own, from_left, from_right, mats[0], mats[2], mats[4]])
    return pl.pallas_call(
        blur_body,
        grid=(VIEWS,),
        out_shape=pltpu.VMEM((VIEWS, ROWS, YE), f32),
        in_specs=[KEPT] * len(operands),
        out_specs=KEPT,
        scratch_shapes=[pltpu.VMEM((ZG, EXR, YE), bf16), pltpu.VMEM((VIEWS, ROWS, YE), bf16)],
        compiler_params=params(),
        cost_estimate=cost(7e9, 1.6e7),
    )(*operands)


def choose(step, codes, code):
    for i, parts in enumerate(codes):

        @pl.when(step == i)
        def _():
            at = 0
            for part in parts:
                rows = slice(at, at + part.shape[0])
                code[rows, :] = part[...]
                at += part.shape[0]


def grouped(refs, layout):
    refs = iter(refs)
    return [[next(refs) for _ in range(n)] for n in layout]


def mirror_body(views, layout, first, last, place, *rest):
    rest = list(rest)
    before = None if first else rest.pop(0)
    codes, rest = grouped(rest, layout), rest[sum(layout) :]
    blur_ref, kxt, tyt, bzt, total = rest[:5]
    code = rest[-1]
    step = pl.program_id(0)
    view = views[0] + (views[-1] - views[0]) * step
    choose(step, codes, code)
    if not first:

        @pl.when(step == 0)
        def _():
            total[...] = before[...]

    quotient = quotient_of(place[1], code[...], blur_ref[view])
    mirrored(quotient, kxt[view], tyt[view], bzt[view], total, first)
    if last:

        @pl.when(step == pl.num_programs(0) - 1)
        def _():
            left, right = rest[5:7]
            send(left, flat(total[:, : EXR // 2]))
            send(right, flat(total[:, EXR // 2 :]))


def mirror(place, before, codes, views, blur_all, mats, last):
    first = before is None
    layout = tuple(len(parts) for parts in codes)
    columns = jax.ShapeDtypeStruct((ZG * EXR // 2 + 16, YE), i16)
    operands = [] if first else [before]
    operands += [part for parts in codes for part in parts]
    operands = kept(operands + [blur_all, mats[1], mats[3], mats[5]])
    return pl.pallas_call(
        functools.partial(mirror_body, views, layout, first, last),
        grid=(len(views),),
        out_shape=(pltpu.VMEM((ZG, EXR, YE), f32),) + (columns,) * (2 * last),
        in_specs=[pl.BlockSpec(memory_space=pltpu.SMEM)] + [KEPT] * len(operands),
        out_specs=(KEPT,) * (1 + 2 * last),
        scratch_shapes=[pltpu.VMEM((ROWS, YE), i16)],
        compiler_params=params(),
        cost_estimate=cost(2e9 * len(views), 8e6 * len(views)),
    )(place, *operands)


def second_body(layout, place, own, e_left, e_right, total, x_left, x_right, *rest):
    codes, rest = grouped(rest, layout), rest[sum(layout) :]
    kx, kxt, ty, tyt, bz, bzt = rest[:6]
    estimate, center, left, right, field, columns, acc, code = rest[6:]
    step = pl.program_id(0)
    edge = MARGIN * ZI
    middle = EXR // 2

    @pl.when(step == 0)
    def _():
        start = widened(own[...], e_left[...], e_right[...]) * (1.0 / VIEWS)
        for half, came in enumerate((x_left, x_right)):
            rows = slice(half * middle, (half + 1) * middle)
            now = start[:, rows] * (total[:, rows] + lane_value(came).reshape(ZG, middle, YE))
            field[:, rows] = now.astype(bf16)
            inner = now[:, edge:] if half == 0 else now[:, : middle - edge]
            estimate[:, half * edge : (half + 1) * edge] = inner[:, :, :YQ]
        blurred_columns(field, kx, columns)
        acc[...] = jnp.zeros_like(acc)

    choose(step, codes, code)
    blur_now = rows_from(blurred(columns[step], ty[step], bz[step]))
    quotient = quotient_of(place[1], code[...], blur_now)
    mirrored(quotient, kxt[step], tyt[step, :, :YQ], bzt[step], acc, False)

    @pl.when(step == pl.num_programs(0) - 1)
    def _():
        center[...] = acc[:, edge : edge + XR, :]
        send(left, flat(acc[:, :edge, :]))
        send(right, flat(acc[:, edge + XR :, :]))


def second(place, own, e_left, e_right, total, x_left, x_right, codes, mats):
    columns = jax.ShapeDtypeStruct((ZG * MARGIN * ZI + 16, YQ), i16)
    cell_shape = pltpu.VMEM((ZG, XR, YQ), f32)
    layout = tuple(len(parts) for parts in codes)
    operands = [own, e_left, e_right, total, x_left, x_right]
    operands += [part for parts in codes for part in parts] + list(mats)
    operands = kept(operands)
    return pl.pallas_call(
        functools.partial(second_body, layout),
        grid=(VIEWS,),
        out_shape=(cell_shape, cell_shape, columns, columns),
        in_specs=[pl.BlockSpec(memory_space=pltpu.SMEM)] + [KEPT] * len(operands),
        out_specs=(KEPT,) * 4,
        scratch_shapes=[
            pltpu.VMEM((ZG, EXR, YE), bf16),
            pltpu.VMEM((VIEWS, ROWS, YE), bf16),
            pltpu.VMEM((ZG, EXR, YQ), f32),
            pltpu.VMEM((ROWS, YE), i16),
        ],
        compiler_params=params(),
        cost_estimate=cost(1.6e10, 4e7),
    )(place, *operands)


def finish_body(estimate, total, x_left, x_right, low, high):
    middle = XR // 2
    a = total[:, :middle] + lane_value(x_left).reshape(ZG, middle, YQ)
    b = total[:, middle:] + lane_value(x_right).reshape(ZG, middle, YQ)
    send(low, flat(estimate[:, :middle] * a * (1.0 / VIEWS)))
    send(high, flat(estimate[:, middle:] * b * (1.0 / VIEWS)))


def finish(estimate, total, x_left, x_right):
    half = jax.ShapeDtypeStruct((ROWS // 2 + 16, YQ), i16)
    return pl.pallas_call(
        finish_body,
        out_shape=(half, half),
        compiler_params=params(),
        cost_estimate=cost(5e6, 4e6),
    )(*kept([estimate, total, x_left, x_right]))


def spread_out(codes, scratch, store):
    middle = XR // 2
    for half in range(2):
        value = lane_value(codes[half])
        for c in range(2):
            scratch[half, c] = value[:, c * 128 : (c + 1) * 128]
            for z in range(NZ):
                rows = pl.ds(z // ZI * middle + z % ZI, BX // 2, stride=ZI)
                store(z, half, c, scratch[half, c, rows, :])


def gather_body(place, *rest):
    codes, out, scratch = rest[: 2 * VIEWS - 2], rest[2 * VIEWS - 2], rest[2 * VIEWS - 1]
    for i, r in enumerate((0, 1, 3)):
        at = lax.rem(place[1] + VIEWS - r, VIEWS) * YQ

        def store(z, half, c, value):
            lanes = pl.ds(pl.multiple_of(at + c * 128, 128), 128)
            out[z, half * BX // 2 : (half + 1) * BX // 2, lanes] = value

        spread_out(codes[2 * i : 2 * i + 2], scratch.at[i], store)


def gathered(place, codes):
    return pl.pallas_call(
        gather_body,
        out_shape=jax.ShapeDtypeStruct((NZ, BX, VIEWS * YQ), f32),
        in_specs=[pl.BlockSpec(memory_space=pltpu.SMEM)] + [KEPT] * len(codes),
        scratch_shapes=[pltpu.VMEM((VIEWS - 1, 2, 2, ROWS // 2, 128), f32)],
        compiler_params=params(),
        cost_estimate=cost(3e6, 6e6),
    )(place, *kept(codes))


def complete_body(place, low, high, _, out, scratch, quarter, sem):
    def store(z, half, c, value):
        quarter[z, half * BX // 2 : (half + 1) * BX // 2, c * 128 : (c + 1) * 128] = value

    spread_out((low, high), scratch, store)
    at = pl.multiple_of(lax.rem(place[1] + 2, VIEWS) * YQ, YQ)
    move = pltpu.make_async_copy(quarter, out.at[:, :, pl.ds(at, YQ)], sem)
    move.start()
    move.wait()


def completed(place, low, high, out):
    anywhere = pl.BlockSpec(memory_space=pl.ANY)
    vmem = pl.BlockSpec(memory_space=pltpu.VMEM)
    return pl.pallas_call(
        complete_body,
        out_shape=jax.ShapeDtypeStruct(out.shape, f32),
        in_specs=[pl.BlockSpec(memory_space=pltpu.SMEM), vmem, vmem, anywhere],
        out_specs=anywhere,
        input_output_aliases={3: 0},
        scratch_shapes=[
            pltpu.VMEM((2, 2, ROWS // 2, 128), f32),
            pltpu.VMEM((NZ, BX, YQ), f32),
            pltpu.SemaphoreType.DMA,
        ],
        compiler_params=params(),
        cost_estimate=cost(1e6, 2e6),
    )(place, *kept([low, high]), out)


def per_device(view_tiles, route_block, route_column, psf_taps, start_estimate):
    groups = lax.axis_size("block")
    cap = max(2, (2 * BX + groups - 1) // groups)
    me, layer = lax.axis_index("block"), lax.axis_index("view")
    place = jnp.stack([me, layer]).astype(i32)

    def around(x, shift):
        return lax.ppermute(x, "view", [(i, (i + shift) % VIEWS) for i in range(VIEWS)])

    def shifted(x, shift):
        pairs = [(i, i + shift) for i in range(groups) if 0 <= i + shift < groups]
        return lax.ppermute(x, "block", pairs)

    outgoing = pack(cap, groups, route_block[0], route_column[0], view_tiles[0])
    arrived = lax.all_to_all(outgoing, "block", split_axis=0, concat_axis=0, tiled=True)

    psf, start_estimate, _ = lax.optimization_barrier((psf_taps[0], start_estimate, outgoing))
    kernel = psf / jnp.sum(psf, axis=1, keepdims=True)
    kernel = kernel.astype(bf16).astype(f32)
    taps = [kernel] + [around(kernel, r) for r in range(1, VIEWS)]
    own, to_left, to_right = cell(place, start_estimate)
    e_left, e_right = shifted(to_right, 1), shifted(to_left, -1)

    codes = unpack(cap, place, arrived)
    own, taps, codes = lax.optimization_barrier((own, taps, codes))
    low_on, high_on = around(codes[2], 1), around(codes[3], -1)
    codes = [
        [codes[0]],
        [around(codes[1], 1)],
        [around(low_on, 1), around(high_on, -1)],
        [around(codes[4], -1)],
    ]
    mats = bands(jnp.stack(taps).reshape(VIEWS, 3 * TAPS))
    blur_all = blur(own, e_left, e_right, mats)
    (total,) = mirror(place, None, codes[:1], [0], blur_all, mats, False)
    (total,) = mirror(place, total, [codes[1], codes[3]], [1, 3], blur_all, mats, False)
    total, left, right = mirror(place, total, codes[2:3], [2], blur_all, mats, True)
    x_left, x_right = shifted(right, 1), shifted(left, -1)
    estimate, center, left, right = second(
        place, own, e_left, e_right, total, x_left, x_right, codes, mats
    )
    x_left, x_right = shifted(right, 1), shifted(left, -1)
    low, high = finish(estimate, center, x_left, x_right)
    low_after, high_before = around(low, -1), around(high, 1)
    high_after, low_before = around(high, -1), around(low, 1)
    low_across, high_across = around(low_after, -1), around(high_before, 1)
    out = gathered(place, [low, high, low_before, high_before, low_after, high_after])
    return completed(place, low_across, high_across, out)


def solution(mesh):
    placed = (
        P("view", "block", None, None),
        P("view", "block"),
        P("view", "block"),
        P("view", None, None),
        P(None, "block", None),
    )
    return jax.shard_map(
        per_device, mesh=mesh, in_specs=placed, out_specs=P(None, "block", None), check_vma=False
    )
```

time: 307 us -> 243 us (0.79); the launches traced: 306 us -> 239 us
  Pallas kernels: 110 us -> 50 us
  waiting for transfers between devices: 140 us -> 118 us
  starting transfers between devices: 47 us -> 68.3 us
  local copies, waits for them, and re-layouts: 6.51 us -> 1.37 us
    pallas_call x10, Pallas kernels: 93.8 us -> 40 us  [the longest x1 10.7 us: second(): pl.pallas_call(functools.partial(second_body, layout), grid=(VIEWS,), out...]
    ppermute x9 -> x15, waiting for transfers between devices: 68.3 us -> 35.4 us  [around(): lax.ppermute(x, 'view', [(i, (i + shift) % VIEWS) for i in range(VIEWS)])]
    all_to_all x1, waiting for transfers between devices: 55.7 us -> 70.5 us  [per_device(): lax.all_to_all(outgoing, 'block', split_axis=0, concat_axis=0, tiled=True)]
    ppermute x9 -> x15, starting transfers between devices: 21.3 us -> 33.2 us  [around(): lax.ppermute(x, 'view', [(i, (i + shift) % VIEWS) for i in range(VIEWS)])]
    ppermute x6, starting transfers between devices: 16.7 us -> 25.8 us  [shifted(): return lax.ppermute(x, 'block', pairs)]
    pallas_call x1, Pallas kernels: 12 us -> 7.01 us  [unpack(): pl.pallas_call(functools.partial(unpack_body, cap, chunk), grid=(groups /...]
    unnamed x24 -> x13, local copies, waits for them, and re-layouts: 5.83 us -> 1.04 us
    ppermute x6, waiting for transfers between devices: 15.9 us -> 12.4 us  [shifted(): return lax.ppermute(x, 'block', pairs)]
  transfers between devices with their start and end apart: 16 -> 22, of which waited for: 8 -> 12; matrix products, arithmetic and copies ran while one was open for 1% -> 0% of each run, Pallas kernels for 24% -> 12%
where the time goes in v2:
time: 243 us; the launch traced here: 239 us
  waiting for transfers between devices  118 us (49%)
  starting transfers between devices  68.3 us (28%)
  Pallas kernels  50 us (21%)
    all_to_all x1, waiting for transfers between devices, per_device(): lax.all_to_all(outgoing, 'block', split_axis=0, concat_axis=0, tiled=True)  70.5 us
    ppermute x15, waiting for transfers between devices, around(): lax.ppermute(x, 'view', [(i, (i + shift) % VIEWS) for i in range(VIEWS)])  35.4 us
    ppermute x15, starting transfers between devices, around(): lax.ppermute(x, 'view', [(i, (i + shift) % VIEWS) for i in range(VIEWS)])  33.2 us
    ppermute x6, starting transfers between devices, shifted(): return lax.ppermute(x, 'block', pairs)  25.8 us
    ppermute x6, waiting for transfers between devices, shifted(): return lax.ppermute(x, 'block', pairs)  12.4 us
    pallas_call x1, Pallas kernels, second(): pl.pallas_call(functools.partial(second_body, layout), grid=(VIEWS,), out...  10.7 us
    all_to_all x1, starting transfers between devices, per_device(): lax.all_to_all(outgoing, 'block', split_axis=0, concat_axis=0, tiled=True)  9.28 us
    pallas_call x3, Pallas kernels, mirror(): pl.pallas_call(functools.partial(mirror_body, views, layout, first, last)...  8.55 us
  transfers between devices with their start and end apart: 22, of which 12 were waited for; matrix products, arithmetic and copies ran while one was open for 0% of the time, Pallas kernels for 12%

profile of v2, /device:TPU:58, one launch (start us, length us, event | category | flops | bytes accessed | tf_op | source)
XLA Modules:
  0.0 238.6 jit_solution(6213652813383640613)
XLA Ops:
  0.0 5.8 %shard_map.55 = bf16[64,400,128]{2,1,0:T(8,128)(2,1)} custom-call(s32[80]{0:T(128)} %bitcast.11, s32[80]{0:T(128)} %bitcast.12, bf16[80,24,1024]{2,1,0:T(8,128)(2,1)} %bitcast.8), custom_call_target="tpu_custom_call" | custom-call | bytes 7864320 | tf_op jit(solution)/shard_map/pallas_call | solution.py:183
  5.8 0.0 copy-start.5
  5.9 0.0 copy-start
  5.9 9.3 %all-to-all-start = ((bf16[64,400,128]{2,1,0:T(8,128)(2,1)}), bf16[64,400,128]{2,1,0:T(8,128)(2,1)}, u32[]{:S(2)}, u32[]{:S(2)}) async-start(bf16[64,400,128]{2,1,0:T(8,128)(2,1)} %shard_map.55), calls=%async_computation | async-start | bytes 13107200 | tf_op jit(solution)/shard_map/all_to_all | solution.py:688
  15.2 0.1 reduce_sum.9
  15.3 0.1 fusion
  15.4 5.4 %collective-permute-start.2 = (f32[3,31]{1,0:T(4,128)S(1)}, f32[3,31]{1,0:T(4,128)S(1)}, u32[]{:S(2)}, u32[]{:S(2)}) collective-permute-start(f32[3,31]{1,0:T(4,128)S(1)} %fusion), channel_id=1, source_target_pairs={{0,192},{64,0},{128,64},{192,128},{1,193},{65,1},{129,65},{193,129... | collective-permute-start | bytes 1124 | tf_op jit(solution)/shard_map/ppermute | solution.py:681
  20.8 1.5 collective-permute-start.1
  22.2 2.4 collective-permute-start
  24.6 0.1 pad_add_fusion.place
  24.7 2.1 shard_map.56
  26.7 1.0 copy-done.1
  27.8 1.9 collective-permute-start.3
  29.7 3.6 %collective-permute-start.4 = (s16[3,128,384]{2,1,0:T(8,128)(2,1)}, s16[3,128,384]{2,1,0:T(8,128)(2,1)S(1)}, u32[]{:S(2)}, u32[]{:S(2)}) collective-permute-start(s16[3,128,384]{2,1,0:T(8,128)(2,1)} %get-tuple-element.50), channel_id=1, source_target_pairs={{1,0},{2,1},{3,2},{4,3},{5,4},{6,5},{7,6},{8,7},{9,8},{10,9},{11,1... | collective-permute-start | bytes 884744 | tf_op jit(solution)/shard_map/ppermute | solution.py:685
  33.3 70.5 %all-to-all-done.arrived.whole_arrived = bf16[64,400,128]{2,1,0:T(8,128)(2,1)} async-done(((bf16[64,400,128]{2,1,0:T(8,128)(2,1)}), bf16[64,400,128]{2,1,0:T(8,128)(2,1)}, u32[]{:S(2)}, u32[]{:S(2)}) %all-to-all-start) | async-done | bytes 6553632 | tf_op jit(solution)/shard_map/all_to_all | solution.py:688
  103.8 7.0 %shard_map.57 = (s16[768,384]{1,0:T(8,128)(2,1)S(1)}, s16[768,384]{1,0:T(8,128)(2,1)S(1)}, s16[384,384]{1,0:T(8,128)(2,1)S(1)}, s16[384,384]{1,0:T(8,128)(2,1)S(1)}, s16[768,384]{1,0:T(8,128)(2,1)S(1)}) custom-call(s32[2]{0:T(128)S(1)} %pad_add_fusion.place, bf16[64,400,128]{2,1,0:T(8,128)(2,1)} %all-to-all-done.arrived.whole_arrived, ...), custom_call_target="tpu_custom_call" | custom-call | flops 3276800 | bytes 6553600 | tf_op jit(solution)/shard_map/pallas_call | solution.py:284
  110.8 0.0 collective-permute-done.2
  110.8 0.0 collective-permute-done.1
  110.8 0.0 collective-permute-done
  110.9 0.1 stack.27
  110.9 0.1 stack.28
  111.0 0.1 stack.29
  111.1 0.1 stack.30
  111.2 3.6 %collective-permute-start.7 = (s16[384,384]{1,0:T(8,128)(2,1)S(1)}, s16[384,384]{1,0:T(8,128)(2,1)S(1)}, u32[]{:S(2)}, u32[]{:S(2)}) collective-permute-start(s16[384,384]{1,0:T(8,128)(2,1)S(1)} %get-tuple-element.64), channel_id=1, source_target_pairs={{0,64},{64,128},{128,192},{192,0},{1,65},{65,129},{129,193},{193,1... | collective-permute-start | bytes 884744 | tf_op jit(solution)/shard_map/ppermute | solution.py:681
  114.8 2.1 collective-permute-start.9
  116.9 1.1 collective-permute-start.5
  118.0 0.0 copy-start.2
  118.0 5.3 %shard_map.58 = (bf16[4,256,512]{2,1,0:T(8,128)(2,1)S(1)}, bf16[4,512,256]{2,1,0:T(8,128)(2,1)S(1)}, bf16[4,384,384]{2,1,0:T(8,128)(2,1)S(1)}, bf16[4,384,384]{2...) custom-call(f32[4,93]{1,0:T(4,128)S(1)} %pad_maximum_fusion.taps), custom_call_target="tpu_custom_call" | custom-call | flops 4000000000 | bytes 20000000 | tf_op jit(solution)/shard_map/pallas_call | solution.py:352
  123.3 0.0 collective-permute-done.3.from_left.e_left
  123.3 3.3 %collective-permute-start.6 = (s16[768,384]{1,0:T(8,128)(2,1)S(1)}, s16[768,384]{1,0:T(8,128)(2,1)S(1)}, u32[]{:S(2)}, u32[]{:S(2)}) collective-permute-start(s16[768,384]{1,0:T(8,128)(2,1)S(1)} %get-tuple-element.63), channel_id=1, source_target_pairs={{0,192},{64,0},{128,64},{192,128},{1,193},{65,1},{129,65},{193,129... | collective-permute-start | bytes 1769480 | tf_op jit(solution)/shard_map/ppermute | solution.py:681
  126.6 5.5 %shard_map.59.rest_1_.rest_3_ = f32[4,768,384]{2,1,0:T(8,128)S(1)} custom-call(f32[3,256,384]{2,1,0:T(8,128)S(1)} %copy-done.2, s16[3,128,384]{2,1,0:T(8,128)(2,1)S(1)} %collective-permute-done.3.from_left.e_left, s16[3,128,384]{2,1,0:T(8,128)(2,1)S(1)} %collective-permute-done.4.from_right.e_right, bf16[4,256,512]{2,1,0:T(8,128)(2,1)S(1)} %get-tuple-element.56.kx.rest_5_, ...), custom_call_target="tpu_custom_call" | custom-call | flops 7000000000 | bytes 16000000 | tf_op jit(solution)/shard_map/pallas_call | solution.py:462
  132.1 2.0 shard_map.60.rest_0_
  134.1 3.4 %collective-permute-done.7 = s16[384,384]{1,0:T(8,128)(2,1)S(1)} collective-permute-done((s16[384,384]{1,0:T(8,128)(2,1)S(1)}, s16[384,384]{1,0:T(8,128)(2,1)S(1)}, u32[]{:S(2)}, u32[]{:S(2)}) %collective-permute-start.7) | collective-permute-done | bytes 294944 | tf_op jit(solution)/shard_map/ppermute | solution.py:681
  137.5 0.6 collective-permute-start.8
  138.2 0.0 collective-permute-done.9
  138.2 3.5 %collective-permute-start.10 = (s16[384,384]{1,0:T(8,128)(2,1)S(1)}, s16[384,384]{1,0:T(8,128)(2,1)S(1)}, u32[]{:S(2)}, u32[]{:S(2)}) collective-permute-start(s16[384,384]{1,0:T(8,128)(2,1)S(1)} %collective-permute-done.9), channel_id=1, source_target_pairs={{0,192},{64,0},{128,64},{192,128},{1,193},{65,1},{129,65},{193,129... | collective-permute-start | bytes 884744 | tf_op jit(solution)/shard_map/ppermute | solution.py:681
  141.7 9.5 %collective-permute-done.5.rest_1_ = s16[768,384]{1,0:T(8,128)(2,1)S(1)} collective-permute-done((s16[768,384]{1,0:T(8,128)(2,1)S(1)}, s16[768,384]{1,0:T(8,128)(2,1)S(1)}, u32[]{:S(2)}, u32[]{:S(2)}) %collective-permute-start.5) | collective-permute-done | bytes 589856 | tf_op jit(solution)/shard_map/ppermute | solution.py:681
  151.2 3.8 %shard_map.61.rest_0_ = f32[3,512,384]{2,1,0:T(8,128)S(1)} custom-call(s32[2]{0:T(128)S(1)} %pad_add_fusion.place, f32[3,512,384]{2,1,0:T(8,128)S(1)} %shard_map.60.rest_0_, s16[768,384]{1,0:T(8,128)(2,1)S(1)} %collective-permute-done.5.rest_1_, s16[768,384]{1,0:T(8,128)(2,1)S(1)} %collective-permute-done.6.rest_2_.rest_4_, ...), custom_call_target="tpu_custom_call" | custom-call | flops 4000000000 | bytes 16000000 | tf_op jit(solution)/shard_map/pallas_call | solution.py:524
  155.0 2.9 %collective-permute-done.8.rest_1_.rest_2_ = s16[384,384]{1,0:T(8,128)(2,1)S(1)} collective-permute-done((s16[384,384]{1,0:T(8,128)(2,1)S(1)}, s16[384,384]{1,0:T(8,128)(2,1)S(1)}, u32[]{:S(2)}, u32[]{:S(2)}) %collective-permute-start.8) | collective-permute-done | bytes 294944 | tf_op jit(solution)/shard_map/ppermute | solution.py:681
  158.0 0.0 collective-permute-done.10.rest_2_.rest_3_
  158.0 2.8 %shard_map.62 = (f32[3,512,384]{2,1,0:T(8,128)S(1)}, s16[784,384]{1,0:T(8,128)(2,1)S(1)}, s16[784,384]{1,0:T(8,128)(2,1)S(1)}) custom-call(s32[2]{0:T(128)S(1)} %pad_add_fusion.place, f32[3,512,384]{2,1,0:T(8,128)S(1)} %shard_map.61.rest_0_, s16[384,384]{1,0:T(8,128)(2,1)S(1)} %collective-permute-done.8.rest_1_.rest_2_, ...), custom_call_target="tpu_custom_call" | custom-call | flops 2000000000 | bytes 8000000 | tf_op jit(solution)/shard_map/pallas_call | solution.py:524
  160.8 1.9 collective-permute-start.11
  162.7 9.5 %collective-permute-start.12 = (s16[784,384]{1,0:T(8,128)(2,1)S(1)}, s16[784,384]{1,0:T(8,128)(2,1)S(1)}, u32[]{:S(2)}, u32[]{:S(2)}) collective-permute-start(s16[784,384]{1,0:T(8,128)(2,1)S(1)} %get-tuple-element.68), channel_id=1, source_target_pairs={{1,0},{2,1},{3,2},{4,3},{5,4},{6,5},{7,6},{8,7},{9,8},{10,9},{11,1... | collective-permute-start | bytes 1806344 | tf_op jit(solution)/shard_map/ppermute | solution.py:685
  172.2 6.8 %collective-permute-done.11.x_left = s16[784,384]{1,0:T(8,128)(2,1)S(1)} collective-permute-done((s16[784,384]{1,0:T(8,128)(2,1)S(1)}, s16[784,384]{1,0:T(8,128)(2,1)S(1)}, u32[]{:S(2)}, u32[]{:S(2)}) %collective-permute-start.11) | collective-permute-done | bytes 602144 | tf_op jit(solution)/shard_map/ppermute | solution.py:685
  179.0 2.4 %collective-permute-done.12.x_right = s16[784,384]{1,0:T(8,128)(2,1)S(1)} collective-permute-done((s16[784,384]{1,0:T(8,128)(2,1)S(1)}, s16[784,384]{1,0:T(8,128)(2,1)S(1)}, u32[]{:S(2)}, u32[]{:S(2)}) %collective-permute-start.12) | collective-permute-done | bytes 602144 | tf_op jit(solution)/shard_map/ppermute | solution.py:685
  181.4 10.7 %shard_map.63 = (f32[3,256,256]{2,1,0:T(8,128)S(1)}, f32[3,256,256]{2,1,0:T(8,128)S(1)}, s16[400,256]{1,0:T(8,128)(2,1)S(1)}, s16[400,256]{1,0:T(8,128)(2,1)S(1)}) custom-call(s32[2]{0:T(128)S(1)} %pad_add_fusion.place, f32[3,256,384]{2,1,0:T(8,128)S(1)} %copy-done.2, s16[3,128,384]{2,1,0:T(8,128)(2,1)S(1)} %collective-permute-done.3.from_left.e_left, ...), custom_call_target="tpu_custom_call" | custom-call | flops 16000000000 | bytes 40000000 | tf_op jit(solution)/shard_map/pallas_call | solution.py:575
  192.1 6.9 %collective-permute-start.13 = (s16[400,256]{1,0:T(8,128)(2,1)S(1)}, s16[400,256]{1,0:T(8,128)(2,1)S(1)}, u32[]{:S(2)}, u32[]{:S(2)}) collective-permute-start(s16[400,256]{1,0:T(8,128)(2,1)S(1)} %get-tuple-element.71), channel_id=1, source_target_pairs={{0,1},{1,2},{2,3},{3,4},{4,5},{5,6},{6,7},{7,8},{8,9},{9,10},{10,1... | collective-permute-start | bytes 614408 | tf_op jit(solution)/shard_map/ppermute | solution.py:685
  199.1 1.9 collective-permute-start.14
  201.0 3.2 %collective-permute-done.14.x_right = s16[400,256]{1,0:T(8,128)(2,1)S(1)} collective-permute-done((s16[400,256]{1,0:T(8,128)(2,1)S(1)}, s16[400,256]{1,0:T(8,128)(2,1)S(1)}, u32[]{:S(2)}, u32[]{:S(2)}) %collective-permute-start.14) | collective-permute-done | bytes 204832 | tf_op jit(solution)/shard_map/ppermute | solution.py:685
  204.2 0.4 shard_map.64
  204.6 1.2 collective-permute-start.15
  205.8 1.9 collective-permute-start.17
  207.7 4.0 %collective-permute-start.19 = (s16[400,256]{1,0:T(8,128)(2,1)S(1)}, s16[400,256]{1,0:T(8,128)(2,1)S(1)}, u32[]{:S(2)}, u32[]{:S(2)}) collective-permute-start(s16[400,256]{1,0:T(8,128)(2,1)S(1)} %get-tuple-element.73.rest_0_), channel_id=1, source_target_pairs={{0,64},{64,128},{128,192},{192,0},{1,65},{65,129},{129,193},{193,1... | collective-permute-start | bytes 614408 | tf_op jit(solution)/shard_map/ppermute | solution.py:681
  211.8 0.1 collective-permute-start.20
  211.9 0.0 collective-permute-done.15.rest_4_
  211.9 2.2 collective-permute-start.16
  214.1 4.8 %collective-permute-done.17.rest_3_ = s16[400,256]{1,0:T(8,128)(2,1)S(1)} collective-permute-done((s16[400,256]{1,0:T(8,128)(2,1)S(1)}, s16[400,256]{1,0:T(8,128)(2,1)S(1)}, u32[]{:S(2)}, u32[]{:S(2)}) %collective-permute-start.17) | collective-permute-done | bytes 204832 | tf_op jit(solution)/shard_map/ppermute | solution.py:681
  218.9 0.3 collective-permute-start.18
  219.2 9.8 %collective-permute-done.19.rest_2_ = s16[400,256]{1,0:T(8,128)(2,1)S(1)} collective-permute-done((s16[400,256]{1,0:T(8,128)(2,1)S(1)}, s16[400,256]{1,0:T(8,128)(2,1)S(1)}, u32[]{:S(2)}, u32[]{:S(2)}) %collective-permute-start.19) | collective-permute-done | bytes 204832 | tf_op jit(solution)/shard_map/ppermute | solution.py:681
  229.0 3.3 %collective-permute-done.20.rest_5_ = s16[400,256]{1,0:T(8,128)(2,1)S(1)} collective-permute-done((s16[400,256]{1,0:T(8,128)(2,1)S(1)}, s16[400,256]{1,0:T(8,128)(2,1)S(1)}, u32[]{:S(2)}, u32[]{:S(2)}) %collective-permute-start.20) | collective-permute-done | bytes 204832 | tf_op jit(solution)/shard_map/ppermute | solution.py:681
  232.3 3.0 %shard_map.65._ = f32[24,32,1024]{2,1,0:T(8,128)} custom-call(s32[2]{0:T(128)S(1)} %pad_add_fusion.place, s16[400,256]{1,0:T(8,128)(2,1)S(1)} %get-tuple-element.73.rest_0_, s16[400,256]{1,0:T(8,128)(2,1)S(1)} %get-tuple-element.74.rest_1_, s16[400,256]{1,0:T(8,128)(2,1)S(1)} %collective-permute-done.19.rest_2_, ...), custom_call_target="tpu_custom_call" | custom-call | flops 3000000 | bytes 6000000 | tf_op jit(solution)/shard_map/pallas_call | solution.py:634
  235.3 1.4 collective-permute-done.16.low
  236.7 0.1 collective-permute-done.18.high
  236.8 1.7 shard_map.66
  (13 shorter events, 0.0 us)
Async XLA Ops:
  5.8 9.3 %copy-start.5 = (f32[1,3,31]{2,0,1:T(1,128)S(1)}, f32[1,3,31]{2,0,1:T(1,128)}, u32[]{:S(2)}) copy-start(f32[1,3,31]{2,0,1:T(1,128)} %param.8) | copy-start | bytes 1120
  5.9 18.8 %copy-start = (f32[24,32,1024]{2,1,0:T(8,128)S(1)}, f32[24,32,1024]{2,1,0:T(8,128)}, u32[]{:S(2)}) copy-start(f32[24,32,1024]{2,1,0:T(8,128)} %start) | copy-start | bytes 9437188
  5.9 97.9 %all-to-all-start = ((bf16[64,400,128]{2,1,0:T(8,128)(2,1)}), bf16[64,400,128]{2,1,0:T(8,128)(2,1)}, u32[]{:S(2)}, u32[]{:S(2)}) async-start(bf16[64,400,128]{2,1,0:T(8,128)(2,1)} %shard_map.55), calls=%async_computation | async-start | bytes 13107200 | tf_op jit(solution)/shard_map/all_to_all | solution.py:688
  15.4 95.5 %collective-permute-start.2 = (f32[3,31]{1,0:T(4,128)S(1)}, f32[3,31]{1,0:T(4,128)S(1)}, u32[]{:S(2)}, u32[]{:S(2)}) collective-permute-start(f32[3,31]{1,0:T(4,128)S(1)} %fusion), channel_id=1, source_target_pairs={{0,192},{64,0},{128,64},{192,128},{1,193},{65,1},{129,65},{193,129... | collective-permute-start | bytes 1124 | tf_op jit(solution)/shard_map/ppermute | solution.py:681
  20.8 90.1 %collective-permute-start.1 = (f32[3,31]{1,0:T(4,128)S(1)}, f32[3,31]{1,0:T(4,128)S(1)}, u32[]{:S(2)}, u32[]{:S(2)}) collective-permute-start(f32[3,31]{1,0:T(4,128)S(1)} %fusion), channel_id=1, source_target_pairs={{0,128},{64,192},{128,0},{192,64},{1,129},{65,193},{129,1},{193,65... | collective-permute-start | bytes 1124 | tf_op jit(solution)/shard_map/ppermute | solution.py:681
  22.2 88.6 %collective-permute-start = (f32[3,31]{1,0:T(4,128)S(1)}, f32[3,31]{1,0:T(4,128)S(1)}, u32[]{:S(2)}, u32[]{:S(2)}) collective-permute-start(f32[3,31]{1,0:T(4,128)S(1)} %fusion), channel_id=1, source_target_pairs={{0,64},{64,128},{128,192},{192,0},{1,65},{65,129},{129,193},{193,1... | collective-permute-start | bytes 1124 | tf_op jit(solution)/shard_map/ppermute | solution.py:681
  26.7 1.0 copy-start.1
  27.8 95.6 %collective-permute-start.3 = (s16[3,128,384]{2,1,0:T(8,128)(2,1)}, s16[3,128,384]{2,1,0:T(8,128)(2,1)S(1)}, u32[]{:S(2)}, u32[]{:S(2)}) collective-permute-start(s16[3,128,384]{2,1,0:T(8,128)(2,1)} %get-tuple-element.49), channel_id=1, source_target_pairs={{0,1},{1,2},{2,3},{3,4},{4,5},{5,6},{6,7},{7,8},{8,9},{9,10},{10,1... | collective-permute-start | bytes 884744 | tf_op jit(solution)/shard_map/ppermute | solution.py:685
  29.7 96.9 %collective-permute-start.4 = (s16[3,128,384]{2,1,0:T(8,128)(2,1)}, s16[3,128,384]{2,1,0:T(8,128)(2,1)S(1)}, u32[]{:S(2)}, u32[]{:S(2)}) collective-permute-start(s16[3,128,384]{2,1,0:T(8,128)(2,1)} %get-tuple-element.50), channel_id=1, source_target_pairs={{1,0},{2,1},{3,2},{4,3},{5,4},{6,5},{7,6},{8,7},{9,8},{10,9},{11,1... | collective-permute-start | bytes 884744 | tf_op jit(solution)/shard_map/ppermute | solution.py:685
  111.2 26.4 %collective-permute-start.7 = (s16[384,384]{1,0:T(8,128)(2,1)S(1)}, s16[384,384]{1,0:T(8,128)(2,1)S(1)}, u32[]{:S(2)}, u32[]{:S(2)}) collective-permute-start(s16[384,384]{1,0:T(8,128)(2,1)S(1)} %get-tuple-element.64), channel_id=1, source_target_pairs={{0,64},{64,128},{128,192},{192,0},{1,65},{65,129},{129,193},{193,1... | collective-permute-start | bytes 884744 | tf_op jit(solution)/shard_map/ppermute | solution.py:681
  114.8 23.4 %collective-permute-start.9 = (s16[384,384]{1,0:T(8,128)(2,1)S(1)}, s16[384,384]{1,0:T(8,128)(2,1)S(1)}, u32[]{:S(2)}, u32[]{:S(2)}) collective-permute-start(s16[384,384]{1,0:T(8,128)(2,1)S(1)} %get-tuple-element.65), channel_id=1, source_target_pairs={{0,192},{64,0},{128,64},{192,128},{1,193},{65,1},{129,65},{193,129... | collective-permute-start | bytes 884744 | tf_op jit(solution)/shard_map/ppermute | solution.py:681
  116.9 34.3 %collective-permute-start.5 = (s16[768,384]{1,0:T(8,128)(2,1)S(1)}, s16[768,384]{1,0:T(8,128)(2,1)S(1)}, u32[]{:S(2)}, u32[]{:S(2)}) collective-permute-start(s16[768,384]{1,0:T(8,128)(2,1)S(1)} %get-tuple-element.62), channel_id=1, source_target_pairs={{0,64},{64,128},{128,192},{192,0},{1,65},{65,129},{129,193},{193,1... | collective-permute-start | bytes 1769480 | tf_op jit(solution)/shard_map/ppermute | solution.py:681
  118.0 8.6 %copy-start.2 = (f32[3,256,384]{2,1,0:T(8,128)S(1)}, f32[3,256,384]{2,1,0:T(8,128)}, u32[]{:S(2)}) copy-start(f32[3,256,384]{2,1,0:T(8,128)} %copy-done.1) | copy-start | bytes 3538948
  123.3 27.9 %collective-permute-start.6 = (s16[768,384]{1,0:T(8,128)(2,1)S(1)}, s16[768,384]{1,0:T(8,128)(2,1)S(1)}, u32[]{:S(2)}, u32[]{:S(2)}) collective-permute-start(s16[768,384]{1,0:T(8,128)(2,1)S(1)} %get-tuple-element.63), channel_id=1, source_target_pairs={{0,192},{64,0},{128,64},{192,128},{1,193},{65,1},{129,65},{193,129... | collective-permute-start | bytes 1769480 | tf_op jit(solution)/shard_map/ppermute | solution.py:681
  126.6 5.5 %copy-start.3 = (s16[3,128,384]{2,1,0:T(8,128)(2,1)}, s16[3,128,384]{2,1,0:T(8,128)(2,1)S(1)}, u32[]{:S(2)}) copy-start(s16[3,128,384]{2,1,0:T(8,128)(2,1)S(1)} %collective-permute-done.4.from_right.e_right) | copy-start | bytes 884740
  137.5 20.4 %collective-permute-start.8 = (s16[384,384]{1,0:T(8,128)(2,1)S(1)}, s16[384,384]{1,0:T(8,128)(2,1)S(1)}, u32[]{:S(2)}, u32[]{:S(2)}) collective-permute-start(s16[384,384]{1,0:T(8,128)(2,1)S(1)} %collective-permute-done.7), channel_id=1, source_target_pairs={{0,64},{64,128},{128,192},{192,0},{1,65},{65,129},{129,193},{193,1... | collective-permute-start | bytes 884744 | tf_op jit(solution)/shard_map/ppermute | solution.py:681
  138.2 19.8 %collective-permute-start.10 = (s16[384,384]{1,0:T(8,128)(2,1)S(1)}, s16[384,384]{1,0:T(8,128)(2,1)S(1)}, u32[]{:S(2)}, u32[]{:S(2)}) collective-permute-start(s16[384,384]{1,0:T(8,128)(2,1)S(1)} %collective-permute-done.9), channel_id=1, source_target_pairs={{0,192},{64,0},{128,64},{192,128},{1,193},{65,1},{129,65},{193,129... | collective-permute-start | bytes 884744 | tf_op jit(solution)/shard_map/ppermute | solution.py:681
  155.0 26.4 %copy-start.4 = (s16[3,128,384]{2,1,0:T(8,128)(2,1)S(1)}, s16[3,128,384]{2,1,0:T(8,128)(2,1)}, u32[]{:S(2)}) copy-start(s16[3,128,384]{2,1,0:T(8,128)(2,1)} %copy-done.3) | copy-start | bytes 884740
  160.8 18.2 %collective-permute-start.11 = (s16[784,384]{1,0:T(8,128)(2,1)S(1)}, s16[784,384]{1,0:T(8,128)(2,1)S(1)}, u32[]{:S(2)}, u32[]{:S(2)}) collective-permute-start(s16[784,384]{1,0:T(8,128)(2,1)S(1)} %get-tuple-element.67), channel_id=1, source_target_pairs={{0,1},{1,2},{2,3},{3,4},{4,5},{5,6},{6,7},{7,8},{8,9},{9,10},{10,1... | collective-permute-start | bytes 1806344 | tf_op jit(solution)/shard_map/ppermute | solution.py:685
  162.7 18.7 %collective-permute-start.12 = (s16[784,384]{1,0:T(8,128)(2,1)S(1)}, s16[784,384]{1,0:T(8,128)(2,1)S(1)}, u32[]{:S(2)}, u32[]{:S(2)}) collective-permute-start(s16[784,384]{1,0:T(8,128)(2,1)S(1)} %get-tuple-element.68), channel_id=1, source_target_pairs={{1,0},{2,1},{3,2},{4,3},{5,4},{6,5},{7,6},{8,7},{9,8},{10,9},{11,1... | collective-permute-start | bytes 1806344 | tf_op jit(solution)/shard_map/ppermute | solution.py:685
  192.1 8.9 %collective-permute-start.13 = (s16[400,256]{1,0:T(8,128)(2,1)S(1)}, s16[400,256]{1,0:T(8,128)(2,1)S(1)}, u32[]{:S(2)}, u32[]{:S(2)}) collective-permute-start(s16[400,256]{1,0:T(8,128)(2,1)S(1)} %get-tuple-element.71), channel_id=1, source_target_pairs={{0,1},{1,2},{2,3},{3,4},{4,5},{5,6},{6,7},{7,8},{8,9},{9,10},{10,1... | collective-permute-start | bytes 614408 | tf_op jit(solution)/shard_map/ppermute | solution.py:685
  199.1 5.2 %collective-permute-start.14 = (s16[400,256]{1,0:T(8,128)(2,1)S(1)}, s16[400,256]{1,0:T(8,128)(2,1)S(1)}, u32[]{:S(2)}, u32[]{:S(2)}) collective-permute-start(s16[400,256]{1,0:T(8,128)(2,1)S(1)} %get-tuple-element.72), channel_id=1, source_target_pairs={{1,0},{2,1},{3,2},{4,3},{5,4},{6,5},{7,6},{8,7},{9,8},{10,9},{11,1... | collective-permute-start | bytes 614408 | tf_op jit(solution)/shard_map/ppermute | solution.py:685
  204.6 7.2 %collective-permute-start.15 = (s16[400,256]{1,0:T(8,128)(2,1)S(1)}, s16[400,256]{1,0:T(8,128)(2,1)S(1)}, u32[]{:S(2)}, u32[]{:S(2)}) collective-permute-start(s16[400,256]{1,0:T(8,128)(2,1)S(1)} %get-tuple-element.73.rest_0_), channel_id=1, source_target_pairs={{0,192},{64,0},{128,64},{192,128},{1,193},{65,1},{129,65},{193,129... | collective-permute-start | bytes 614408 | tf_op jit(solution)/shard_map/ppermute | solution.py:681
  205.8 13.1 %collective-permute-start.17 = (s16[400,256]{1,0:T(8,128)(2,1)S(1)}, s16[400,256]{1,0:T(8,128)(2,1)S(1)}, u32[]{:S(2)}, u32[]{:S(2)}) collective-permute-start(s16[400,256]{1,0:T(8,128)(2,1)S(1)} %get-tuple-element.74.rest_1_), channel_id=1, source_target_pairs={{0,64},{64,128},{128,192},{192,0},{1,65},{65,129},{129,193},{193,1... | collective-permute-start | bytes 614408 | tf_op jit(solution)/shard_map/ppermute | solution.py:681
  207.7 21.3 %collective-permute-start.19 = (s16[400,256]{1,0:T(8,128)(2,1)S(1)}, s16[400,256]{1,0:T(8,128)(2,1)S(1)}, u32[]{:S(2)}, u32[]{:S(2)}) collective-permute-start(s16[400,256]{1,0:T(8,128)(2,1)S(1)} %get-tuple-element.73.rest_0_), channel_id=1, source_target_pairs={{0,64},{64,128},{128,192},{192,0},{1,65},{65,129},{129,193},{193,1... | collective-permute-start | bytes 614408 | tf_op jit(solution)/shard_map/ppermute | solution.py:681
  211.8 20.6 %collective-permute-start.20 = (s16[400,256]{1,0:T(8,128)(2,1)S(1)}, s16[400,256]{1,0:T(8,128)(2,1)S(1)}, u32[]{:S(2)}, u32[]{:S(2)}) collective-permute-start(s16[400,256]{1,0:T(8,128)(2,1)S(1)} %get-tuple-element.74.rest_1_), channel_id=1, source_target_pairs={{0,192},{64,0},{128,64},{192,128},{1,193},{65,1},{129,65},{193,129... | collective-permute-start | bytes 614408 | tf_op jit(solution)/shard_map/ppermute | solution.py:681
  211.9 24.8 %collective-permute-start.16 = (s16[400,256]{1,0:T(8,128)(2,1)S(1)}, s16[400,256]{1,0:T(8,128)(2,1)S(1)}, u32[]{:S(2)}, u32[]{:S(2)}) collective-permute-start(s16[400,256]{1,0:T(8,128)(2,1)S(1)} %collective-permute-done.15.rest_4_), channel_id=1, source_target_pairs={{0,192},{64,0},{128,64},{192,128},{1,193},{65,1},{129,65},{193,129... | collective-permute-start | bytes 614408 | tf_op jit(solution)/shard_map/ppermute | solution.py:681
  218.9 17.9 %collective-permute-start.18 = (s16[400,256]{1,0:T(8,128)(2,1)S(1)}, s16[400,256]{1,0:T(8,128)(2,1)S(1)}, u32[]{:S(2)}, u32[]{:S(2)}) collective-permute-start(s16[400,256]{1,0:T(8,128)(2,1)S(1)} %collective-permute-done.17.rest_3_), channel_id=1, source_target_pairs={{0,64},{64,128},{128,192},{192,0},{1,65},{65,129},{129,193},{193,1... | collective-permute-start | bytes 614408 | tf_op jit(solution)/shard_map/ppermute | solution.py:681
